TPU v7x, 32 devices: a whole 2x2x4 slice. The times are simulated.
32 devices in a mesh: dp: 4 (over x, core), head: 2 (over y), hidden: 4 (over z).
Axes of the slice: x: 2, y: 2, z: 4, core: 2. Of those that a mesh axis runs over, the one named last changes fastest.
Arguments:
- tokens: bfloat16 [16, 512, 1024], P(('dp', 'hidden'), 'head'), may hold values from -6 to 6
- lengths: int32 [16, 1], P(('dp', 'hidden')), may hold values from 449 to 512, as said below
- norm_first: float32 [1024], replicated, may hold values from 0.5 to 1.5
- w_qkv: bfloat16 [1024, 3, 1024], P(None, None, 'head'), may hold values from -0.1875 to 0.1875
- w_feature: bfloat16 [2, 16, 64, 64], P(None, 'head'), may hold values from -1.5 to 1.5
- w_out: bfloat16 [1024, 1024], P('head'), may hold values from -2 to 2
- norm_second: float32 [1024], replicated, may hold values from 0.5 to 1.5
- w_up: bfloat16 [1024, 4096], P(None, 'hidden'), may hold values from -0.1875 to 0.1875
- w_down: bfloat16 [4096, 1024], P('hidden'), may hold values from -0.09375 to 0.09375
- cotangent: bfloat16 [16, 512, 1024], P(('dp', 'hidden'), 'head'), may hold values from -6 to 6
Outputs:
- block_out: bfloat16 [16, 512, 1024], P(('dp', 'hidden'), 'head')
- grad_tokens: float32 [16, 512, 1024], P(('dp', 'hidden'), 'head')
- grad_norm_first: float32 [1024], replicated
- grad_qkv: float32 [1024, 3, 1024], P(None, None, 'head')
- grad_feature: float32 [2, 16, 64, 64], P(None, 'head')
- grad_out: float32 [1024, 1024], P('head')
- grad_norm_second: float32 [1024], replicated
- grad_up: float32 [1024, 4096], P(None, 'hidden')
- grad_down: float32 [4096, 1024], P('hidden')
Inputs may be any that keep to these rules, and one draw needn't show every extreme that they name: `lengths`: each bin holds a single sequence, padded up to whole blocks of 64 tokens, that fills the 512 slots of its bin exactly. In every draw some bin holds a sequence of exactly 512 tokens.
All inputs are finite; a program needn't handle non-finite values.
Results may differ from a plain program's by a relative error of at most 0.019.
Values may be sent and summed in bfloat16 or wider, within the bound.
A program may use at most 192 MiB of HBM per device.

v0:
```python
import jax
import jax.numpy as jnp
from jax import lax
from jax.sharding import PartitionSpec as P

BLOCK = 64


EPS = 1e-05
HIGH = lax.Precision.HIGHEST


def normalize(values, gain):
    average = jnp.mean(values, axis=-1, keepdims=True)
    centred = values - average
    spread = jnp.mean(centred * centred, axis=-1, keepdims=True)
    return centred * lax.rsqrt(spread + EPS) * gain


def hedgehog_map(logits):
    return jnp.concatenate(
        [jax.nn.softmax(logits, axis=-1), jax.nn.softmax(-logits, axis=-1)], axis=-1
    )


def feature_back(logits, grad):
    half = logits.shape[-1]
    first = jax.nn.softmax(logits, axis=-1)
    second = jax.nn.softmax(-logits, axis=-1)
    grad_first = grad[..., :half]
    grad_second = grad[..., half:]
    part_first = first * (grad_first - jnp.sum(first * grad_first, axis=-1, keepdims=True))
    part_second = second * (grad_second - jnp.sum(second * grad_second, axis=-1, keepdims=True))
    return part_first - part_second


def smooth_gate(values):
    return jax.nn.gelu(values, approximate=True)


def packing(lengths, row_count, block_len):
    padded = (lengths + block_len - 1) // block_len * block_len
    ends = jnp.cumsum(padded)
    starts = ends - padded
    slots = jnp.arange(row_count, dtype=jnp.int32)
    segment = jnp.sum((ends[None, :] <= slots[:, None]).astype(jnp.int32), axis=1)
    member = segment[:, None] == jnp.arange(lengths.shape[0], dtype=jnp.int32)[None, :]
    begin = jnp.sum(jnp.where(member, starts[None, :], 0), axis=1)
    extent = jnp.sum(jnp.where(member, lengths[None, :], 0), axis=1)
    valid = (slots - begin < extent).astype(jnp.float32)
    block_count = row_count // block_len
    block_segment = segment.reshape(block_count, block_len)[:, 0]
    blocks = jnp.arange(block_count, dtype=jnp.int32)
    earlier = (blocks[None, :] < blocks[:, None]) & (
        block_segment[None, :] == block_segment[:, None]
    )
    return (valid, earlier.astype(jnp.float32))


def attend_parts(projected, w_feature, valid, earlier):
    row_count = projected.shape[0]
    head_count = w_feature.shape[1]
    head_size = w_feature.shape[2]
    block_count = earlier.shape[0]
    block_len = row_count // block_count
    query, key, value = (projected[:, 0], projected[:, 1], projected[:, 2])
    u_query = jnp.einsum("nhd,hde->nhe", query, w_feature[0], preferred_element_type=jnp.float32)
    u_key = jnp.einsum("nhd,hde->nhe", key, w_feature[1], preferred_element_type=jnp.float32)
    f_query = (
        hedgehog_map(u_query)
        .astype(jnp.bfloat16)
        .reshape(block_count, block_len, head_count, 2 * head_size)
    )
    f_key = (hedgehog_map(u_key) * valid[:, None, None]).astype(jnp.bfloat16)
    f_key = f_key.reshape(block_count, block_len, head_count, 2 * head_size)
    value_blocks = value.reshape(block_count, block_len, head_count, head_size)
    lower_mask = (jnp.arange(block_len)[:, None] >= jnp.arange(block_len)[None, :]).astype(
        jnp.float32
    )
    scores = (
        jnp.einsum("cihf,cjhf->chij", f_query, f_key, preferred_element_type=jnp.float32)
        * lower_mask
    )
    scores_low = scores.astype(jnp.bfloat16)
    inner = jnp.einsum(
        "chij,cjhd->cihd", scores_low, value_blocks, preferred_element_type=jnp.float32
    )
    inner_sum = jnp.transpose(jnp.sum(scores, axis=-1), (0, 2, 1))
    states = jnp.einsum("cjhf,cjhd->chfd", f_key, value_blocks, preferred_element_type=jnp.float32)
    key_sums = jnp.sum(f_key.astype(jnp.float32), axis=1)
    prior_low = jnp.einsum("ce,ehfd->chfd", earlier, states, precision=HIGH).astype(jnp.bfloat16)
    prior_sum = jnp.einsum("ce,ehf->chf", earlier, key_sums, precision=HIGH)
    outer = jnp.einsum("cihf,chfd->cihd", f_query, prior_low, preferred_element_type=jnp.float32)
    outer_sum = jnp.einsum("cihf,chf->cih", f_query.astype(jnp.float32), prior_sum, precision=HIGH)
    numer = inner + outer
    denom = inner_sum + outer_sum
    return (
        u_query,
        u_key,
        f_query,
        f_key,
        value_blocks,
        lower_mask,
        scores_low,
        prior_low,
        prior_sum,
        numer,
        denom,
    )


def mixed_of(parts, row_count):
    numer, denom = (parts[9], parts[10])
    return (numer / denom[..., None]).reshape(row_count, -1).astype(jnp.bfloat16)


def attend_back(projected, w_feature, valid, earlier, d_mixed):
    row_count = projected.shape[0]
    head_count = w_feature.shape[1]
    head_size = w_feature.shape[2]
    parts = attend_parts(projected, w_feature, valid, earlier)
    (
        u_query,
        u_key,
        f_query,
        f_key,
        value_blocks,
        lower_mask,
        scores_low,
        prior_low,
        prior_sum,
        numer,
        denom,
    ) = parts
    block_count, block_len = (f_query.shape[0], f_query.shape[1])
    d_att = d_mixed.reshape(block_count, block_len, head_count, head_size)
    d_numer = (d_att / denom[..., None]).astype(jnp.bfloat16)
    d_denom = -jnp.sum(d_att * numer, axis=-1) / (denom * denom)
    query_wide = f_query.astype(jnp.float32)
    d_fq = jnp.einsum("cihd,chfd->cihf", d_numer, prior_low, preferred_element_type=jnp.float32)
    d_fq = d_fq + d_denom[..., None] * prior_sum[:, None, :, :]
    d_prior = jnp.einsum("cihf,cihd->chfd", f_query, d_numer, preferred_element_type=jnp.float32)
    d_prior_sum = jnp.einsum("cihf,cih->chf", query_wide, d_denom, precision=HIGH)
    d_states = jnp.einsum("ce,chfd->ehfd", earlier, d_prior, precision=HIGH).astype(jnp.bfloat16)
    d_key_sums = jnp.einsum("ce,chf->ehf", earlier, d_prior_sum, precision=HIGH)
    d_scores = jnp.einsum(
        "cihd,cjhd->chij", d_numer, value_blocks, preferred_element_type=jnp.float32
    )
    d_scores = ((d_scores + jnp.transpose(d_denom, (0, 2, 1))[..., None]) * lower_mask).astype(
        jnp.bfloat16
    )
    d_fk = jnp.einsum("cjhd,chfd->cjhf", value_blocks, d_states, preferred_element_type=jnp.float32)
    d_fk = (
        d_fk
        + d_key_sums[:, None]
        + jnp.einsum("chij,cihf->cjhf", d_scores, f_query, preferred_element_type=jnp.float32)
    )
    d_fq = d_fq + jnp.einsum("chij,cjhf->cihf", d_scores, f_key, preferred_element_type=jnp.float32)
    d_value = jnp.einsum("cjhf,chfd->cjhd", f_key, d_states, preferred_element_type=jnp.float32)
    d_value = d_value + jnp.einsum(
        "chij,cihd->cjhd", scores_low, d_numer, preferred_element_type=jnp.float32
    )
    d_fq = d_fq.reshape(row_count, head_count, 2 * head_size)
    d_fk = d_fk.reshape(row_count, head_count, 2 * head_size) * valid[:, None, None]
    du_query = feature_back(u_query, d_fq).astype(jnp.bfloat16)
    du_key = feature_back(u_key, d_fk).astype(jnp.bfloat16)
    query, key = (projected[:, 0], projected[:, 1])
    grad_feature = jnp.stack(
        [
            jnp.einsum("nhd,nhe->hde", query, du_query, preferred_element_type=jnp.float32),
            jnp.einsum("nhd,nhe->hde", key, du_key, preferred_element_type=jnp.float32),
        ]
    )
    d_query = jnp.einsum("nhe,hde->nhd", du_query, w_feature[0], preferred_element_type=jnp.float32)
    d_key = jnp.einsum("nhe,hde->nhd", du_key, w_feature[1], preferred_element_type=jnp.float32)
    d_projected = jnp.stack(
        [d_query, d_key, d_value.reshape(row_count, head_count, head_size)], axis=1
    )
    d_projected = d_projected.astype(jnp.bfloat16).reshape(row_count, -1)
    return (d_projected, grad_feature, mixed_of(parts, row_count))


def per_device(
    tokens, lengths, norm_first, w_qkv, w_feature, w_out, norm_second, w_up, w_down, cotangent
):
    width = tokens.shape[2]
    head_count = w_feature.shape[1]
    head_size = w_feature.shape[2]
    qkv_flat = w_qkv.reshape(width, -1)
    residual_in = tokens[0].astype(jnp.float32)
    normed_first, first_back = jax.vjp(normalize, residual_in, norm_first)
    first_low = normed_first.astype(jnp.bfloat16)
    first_rows = lax.all_gather(first_low, "head", axis=0, tiled=True)
    bin_rows = first_rows.shape[0]
    valid, earlier = packing(lengths[0], bin_rows, BLOCK)
    projected = jnp.dot(first_rows, qkv_flat, preferred_element_type=jnp.float32).astype(
        jnp.bfloat16
    )
    projected = projected.reshape(bin_rows, 3, head_count, head_size)
    mixed_low = mixed_of(attend_parts(projected, w_feature, valid, earlier), bin_rows)
    branch = lax.psum_scatter(
        jnp.dot(mixed_low, w_out, preferred_element_type=jnp.float32),
        "head",
        scatter_dimension=0,
        tiled=True,
    )
    middle = residual_in + branch
    normed_second, second_back = jax.vjp(normalize, middle, norm_second)
    second_low = normed_second.astype(jnp.bfloat16)
    cot_low = cotangent[0]
    second_rows = lax.all_gather(second_low, "hidden", axis=0, tiled=True)
    hidden_pre = jnp.dot(second_rows, w_up, preferred_element_type=jnp.float32)
    active = smooth_gate(hidden_pre).astype(jnp.bfloat16)
    mlp_result = lax.psum_scatter(
        jnp.dot(active, w_down, preferred_element_type=jnp.float32).astype(jnp.bfloat16),
        "hidden",
        scatter_dimension=0,
        tiled=True,
    ).astype(jnp.float32)
    block_out = (middle + mlp_result).astype(jnp.bfloat16)
    gate_grad = jax.vjp(smooth_gate, hidden_pre)[1]
    cot_rows = lax.all_gather(cot_low, "hidden", axis=0, tiled=True)
    grad_down = jnp.einsum("nf,nd->fd", active, cot_rows, preferred_element_type=jnp.float32)
    d_active = jnp.einsum("nd,fd->nf", cot_rows, w_down, preferred_element_type=jnp.float32)
    d_pre = gate_grad(d_active)[0].astype(jnp.bfloat16)
    grad_up = jnp.einsum("nd,nf->df", second_rows, d_pre, preferred_element_type=jnp.float32)
    piece = d_pre
    d_second = lax.psum_scatter(
        jnp.einsum("nf,df->nd", piece, w_up, preferred_element_type=jnp.float32),
        "hidden",
        scatter_dimension=0,
        tiled=True,
    )
    d_middle_norm, grad_norm_second = second_back(d_second)
    d_middle = cot_low.astype(jnp.float32) + d_middle_norm
    d_branch_low = d_middle.astype(jnp.bfloat16)
    kept_rows, d_branch_rows = (
        lax.all_gather(first_low, "head", axis=0, tiled=True),
        lax.all_gather(d_branch_low, "head", axis=0, tiled=True),
    )
    kept_projected = jnp.dot(kept_rows, qkv_flat, preferred_element_type=jnp.float32).astype(
        jnp.bfloat16
    )
    kept_projected = kept_projected.reshape(bin_rows, 3, head_count, head_size)
    d_att = jnp.einsum("nd,kd->nk", d_branch_rows, w_out, preferred_element_type=jnp.float32)
    d_projected, grad_feature, mixed_again = attend_back(
        kept_projected, w_feature, valid, earlier, d_att
    )
    grad_out = jnp.einsum(
        "nk,nd->kd", mixed_again, d_branch_rows, preferred_element_type=jnp.float32
    )
    grad_qkv = jnp.einsum(
        "nd,nk->dk", kept_rows, d_projected, preferred_element_type=jnp.float32
    ).reshape(w_qkv.shape)
    piece = d_projected
    d_first = lax.psum_scatter(
        jnp.einsum("nk,dk->nd", piece, qkv_flat, preferred_element_type=jnp.float32).astype(
            jnp.bfloat16
        ),
        "head",
        scatter_dimension=0,
        tiled=True,
    ).astype(jnp.float32)
    d_input_norm, grad_norm_first = first_back(d_first)
    grad_tokens = d_middle + d_input_norm
    grad_qkv, grad_feature, grad_out = (
        lax.psum(grad_qkv.astype(jnp.bfloat16), ("dp", "hidden")).astype(jnp.float32),
        lax.psum(grad_feature.astype(jnp.bfloat16), ("dp", "hidden")).astype(jnp.float32),
        lax.psum(grad_out.astype(jnp.bfloat16), ("dp", "hidden")).astype(jnp.float32),
    )
    grad_up, grad_down = (
        lax.psum(grad_up.astype(jnp.bfloat16), ("dp", "head")).astype(jnp.float32),
        lax.psum(grad_down.astype(jnp.bfloat16), ("dp", "head")).astype(jnp.float32),
    )
    grad_norm_first, grad_norm_second = lax.psum(
        (grad_norm_first, grad_norm_second), ("dp", "head", "hidden")
    )
    return (
        block_out[None],
        grad_tokens[None],
        grad_norm_first,
        grad_qkv,
        grad_feature,
        grad_out,
        grad_norm_second,
        grad_up,
        grad_down,
    )


def solution(mesh):
    in_specs = (
        P(("dp", "hidden"), "head", None),
        P(("dp", "hidden"), None),
        P(),
        P(None, None, "head"),
        P(None, "head", None, None),
        P("head", None),
        P(),
        P(None, "hidden"),
        P("hidden", None),
        P(("dp", "hidden"), "head", None),
    )
    out_specs = (
        P(("dp", "hidden"), "head", None),
        P(("dp", "hidden"), "head", None),
        P(),
        P(None, None, "head"),
        P(None, "head", None, None),
        P("head", None),
        P(),
        P(None, "hidden"),
        P("hidden", None),
    )
    return jax.shard_map(
        per_device, mesh=mesh, in_specs=in_specs, out_specs=out_specs, check_vma=False
    )
```

profile of v0, /device:TPU:0, one launch (start us, length us, event | category | flops | bytes accessed | tf_op | source)
XLA Modules:
  0.0 634.3 jit_solution(11833460381632394299)
XLA Ops:
  12.9 4.6 copy.88
  17.6 18.7 %all-gather.6.cloned.1.call-done = bf16[512,1024]{1,0:T(8,128)(2,1)} async-done(((bf16[256,1024]{1,0:T(8,128)(2,1)}), bf16[512,1024]{1,0:T(8,128)(2,1)}) %all-gather.6.cloned.1.call-update) | async-done | bytes 1048592 | tf_op jit(solution)/shard_map/all_gather | solution.py:193
  36.3 5.2 convolution_convert_fusion
  77.3 3.1 copy.94
  80.3 3.0 convert_reduce_fusion
  98.3 3.4 fusion.173
  101.8 31.9 %reduce-scatter.5.cloned.1.call-done = f32[256,1024]{1,0:T(8,128)} async-done(((f32[512,1024]{1,0:T(8,128)}), f32[256,1024]{1,0:T(8,128)}) %reduce-scatter.5.cloned.1.call-update) | async-done | bytes 1048592 | tf_op jit(solution)/shard_map/reduce_scatter | solution.py:201
  138.3 45.0 %all-gather.8.cloned.1.call-done = bf16[1024,1024]{1,0:T(8,128)(2,1)} async-done(((bf16[256,1024]{1,0:T(8,128)(2,1)}), bf16[1024,1024]{1,0:T(8,128)(2,1)}) %all-gather.8.cloned.1.call-update) | async-done | bytes 2097168 | tf_op jit(solution)/shard_map/all_gather | solution.py:211
  183.3 5.9 fusion.174
  189.3 40.3 %all-gather.12.cloned.1.call-done = bf16[1,1024,1024]{2,1,0:T(8,128)(2,1)} async-done(((bf16[1,256,1024]{2,1,0:T(8,128)(2,1)}), bf16[1,1024,1024]{2,1,0:T(8,128)(2,1)}) %all-gather.12.cloned.1.call-update) | async-done | bytes 2097168 | tf_op jit(solution)/shard_map/all_gather | solution.py:222
  229.5 8.0 %fusion.18 = bf16[1024,1024]{1,0:T(8,128)(2,1)S(1)} fusion(f32[1024,1024]{1,0:T(8,128)} %fusion.174, bf16[1024,1024]{1,0:T(8,128)(2,1)} %param.18, bf16[1,1024,1024]{2,1,0:T(8,128)(2,1)} %all-gather.12.cloned.1.call-done), kind=kOutput, calls=%fused_computation.20 | convolution fusion | flops 2168455168 | bytes 10485760 | tf_op jit(solution)/shard_map/nd,fd->nf/dot_general | solution.py:224
  238.8 4.4 fusion.175
  244.8 6.1 convolution_convert_fusion.3
  251.7 67.2 %reduce-scatter.9.cloned.1.call-done = f32[256,1024]{1,0:T(8,128)} async-done(((f32[1024,1024]{1,0:T(8,128)}), f32[256,1024]{1,0:T(8,128)}) %reduce-scatter.9.cloned.1.call-update) | async-done | bytes 1048592 | tf_op jit(solution)/shard_map/reduce_scatter | solution.py:228
  321.6 43.8 %reduce-scatter.7.cloned.1.call-done = bf16[256,1024]{1,0:T(8,128)(2,1)} async-done(((bf16[1024,1024]{1,0:T(8,128)(2,1)}), bf16[256,1024]{1,0:T(8,128)(2,1)}) %reduce-scatter.7.cloned.1.call-update) | async-done | bytes 524304 | tf_op jit(solution)/shard_map/reduce_scatter | solution.py:214
  369.4 6.1 convolution_convert_fusion.2
  375.5 4.1 fusion.32
  379.7 10.3 %all-gather.10.cloned.1.call-done = bf16[512,1024]{1,0:T(8,128)(2,1)} async-done(((bf16[256,1024]{1,0:T(8,128)(2,1)}), bf16[512,1024]{1,0:T(8,128)(2,1)}) %all-gather.10.cloned.1.call-update) | async-done | bytes 1048592 | tf_op jit(solution)/shard_map/all_gather | solution.py:239
  396.3 3.0 fusion.27
  418.7 3.1 copy.124
  424.4 3.2 copy.151
  427.6 3.3 copy.152
  433.6 3.4 convolution_bitcast_fusion
  439.0 3.7 convolution_bitcast_fusion.1
  454.9 3.5 convolution_convert_fusion.5
  458.4 3.5 convolution_convert_fusion.1
  462.0 12.9 %all-reduce.8.cloned.1.call-done = (bf16[1024,1024]{1,0:T(8,128)(2,1)}, bf16[1024,1024]{1,0:T(8,128)(2,1)}) async-done(((bf16[1024,1024]{1,0:T(8,128)(2,1)}, bf16[1024,1024]{1,0:T(8,128)(2,1)}), (bf16[1024,1024]{1,0:T(8,128)(2,1)}, bf16[1024,1024]{1,0:T(8,128)(2,1)})) %all-reduce.8.cloned.1.call-update) | async-done | bytes 4194320 | tf_op jit(solution)/shard_map/psum | solution.py:272
  474.8 4.2 convert_element_type.208
  481.6 16.5 %reduce-scatter.11.cloned.1.call-done = bf16[256,1024]{1,0:T(8,128)(2,1)} async-done(((bf16[512,1024]{1,0:T(8,128)(2,1)}), bf16[256,1024]{1,0:T(8,128)(2,1)}) %reduce-scatter.11.cloned.1.call-update) | async-done | bytes 524304 | tf_op jit(solution)/shard_map/reduce_scatter | solution.py:256
  501.2 40.9 %all-reduce = (f32[1024]{0:T(1024)}, f32[1024]{0:T(1024)}) all-reduce(f32[1024]{0:T(1024)S(1)} %get-tuple-element.11, f32[1024]{0:T(1024)S(1)} %copy-done.44), channel_id=1, replica_groups=mesh['dp'=4,'head'=2,'hidden'=4] {'dp','head','hidden'}, use_global_device_ids=true, to_apply=%region_28.29 | all-reduce | flops 2048 | bytes 16384 | tf_op jit(solution)/shard_map/psum | solution.py:275
  543.6 75.0 %all-reduce.6.cloned.1.call-done = (bf16[1024,3,512]{2,0,1:T(8,128)(2,1)}, bf16[2,8,64,64]{3,2,1,0:T(8,128)(2,1)}, bf16[512,1024]{1,0:T(8,128)(2,1)}) async-done(((bf16[1024,3,512]{2,0,1:T(8,128)(2,1)}, bf16[2,8,64,64]{3,2,1,0:T(8,128)(2,1)}, bf16[512,1024]{1,0:T(8,128)(2,1)}), (bf16[1024,3,512]{2,0,1:T(8,128)(2,1)}, bf16[2,8,64,64]{3,2,1,0:T(8,128)(2,1)}, ...) | async-done | bytes 4325392 | tf_op jit(solution)/shard_map/psum | solution.py:267
  623.4 3.6 convert_element_type.203
  (223 shorter events, 127.4 us)
Async XLA Ops:
  7.2 176.1 %copy-start = (bf16[1024,1024]{1,0:T(8,128)(2,1)S(1)}, bf16[1024,1024]{1,0:T(8,128)(2,1)}, u32[]{:S(2)}) copy-start(bf16[1024,1024]{1,0:T(8,128)(2,1)} %param.17) | copy-start | bytes 6291460
  7.2 29.1 %all-gather.6.cloned.1.call-start = ((), (), s32[]{:S(2)}) async-start(), calls=%async_computation.4 | async-start | bytes 1572864 | tf_op jit(solution)/shard_map/all_gather | solution.py:193
  12.1 121.6 %reduce-scatter.5.cloned.1.call-start = ((), (), s32[]{:S(2)}) async-start(), calls=%async_computation.5 | async-start | bytes 3145728 | tf_op jit(solution)/shard_map/reduce_scatter | solution.py:201
  83.3 5.5 copy-start.4
  101.7 34.5 %copy-start.43 = (f32[1024]{0:T(1024)S(1)}, f32[1024]{0:T(1024)}, u32[]{:S(2)}) copy-start(f32[1024]{0:T(1024)} %param.16) | copy-start | bytes 12292
  101.7 81.6 %all-gather.8.cloned.1.call-start = ((), (), s32[]{:S(2)}) async-start(), calls=%async_computation.6 | async-start | bytes 2621440 | tf_op jit(solution)/shard_map/all_gather | solution.py:211
  135.5 53.8 %copy-start.51 = (f32[256]{0:T(256)}, f32[256]{0:T(256)S(1)}, u32[]{:S(2)}) copy-start(f32[256]{0:T(256)S(1)} %multiply_reduce_fusion.3) | copy-start | bytes 3076
  136.2 53.0 %copy-start.45 = (f32[256]{0:T(256)}, f32[256]{0:T(256)S(1)}, u32[]{:S(2)}) copy-start(f32[256]{0:T(256)S(1)} %fusion.143) | copy-start | bytes 3076
  137.2 92.3 %all-gather.12.cloned.1.call-start = ((), (), s32[]{:S(2)}) async-start(), calls=%async_computation.11 | async-start | bytes 2621440 | tf_op jit(solution)/shard_map/all_gather | solution.py:222
  137.8 181.0 %reduce-scatter.9.cloned.1.call-start = ((), (), s32[]{:S(2)}) async-start(), calls=%async_computation.8 | async-start | bytes 5242880 | tf_op jit(solution)/shard_map/reduce_scatter | solution.py:228
  243.2 122.2 %reduce-scatter.7.cloned.1.call-start = ((), (), s32[]{:S(2)}) async-start(), calls=%async_computation.7 | async-start | bytes 2621440 | tf_op jit(solution)/shard_map/reduce_scatter | solution.py:214
  250.9 67.9 %copy-start.3 = (f32[256,1024]{1,0:T(8,128)S(1)}, f32[256,1024]{1,0:T(8,128)}, u32[]{:S(2)}) copy-start(f32[256,1024]{1,0:T(8,128)} %copy-done.2) | copy-start | bytes 3145732
  250.9 67.9 %copy-start.46 = (f32[256]{0:T(256)S(1)}, f32[256]{0:T(256)}, u32[]{:S(2)}) copy-start(f32[256]{0:T(256)} %copy-done.45) | copy-start | bytes 3076
  250.9 70.1 %copy-start.52 = (f32[256]{0:T(256)S(1)}, f32[256]{0:T(256)}, u32[]{:S(2)}) copy-start(f32[256]{0:T(256)} %copy-done.51) | copy-start | bytes 3076
  250.9 139.0 %all-gather.10.cloned.1.call-start = ((), (), s32[]{:S(2)}) async-start(), calls=%async_computation.9 | async-start | bytes 1572864 | tf_op jit(solution)/shard_map/all_gather | solution.py:239
  368.0 7.5 %copy-start.15 = (f32[256,1024]{1,0:T(8,128)}, f32[256,1024]{1,0:T(8,128)S(1)}, u32[]{:S(2)}) copy-start(f32[256,1024]{1,0:T(8,128)S(1)} %get-tuple-element.21) | copy-start | bytes 3145732
  369.2 105.7 %all-reduce.8.cloned.1.call-start = ((), (), s32[]{:S(2)}) async-start(), calls=%async_computation.13 | async-start | bytes 8388608 | tf_op jit(solution)/shard_map/psum | solution.py:272
  369.4 6.1 copy-start.55
  369.4 6.1 copy-start.57
  379.6 10.3 %copy-start.36 = (bf16[512,1024]{1,0:T(8,128)(2,1)S(1)}, bf16[512,1024]{1,0:T(8,128)(2,1)}, u32[]{:S(2)}) copy-start(bf16[512,1024]{1,0:T(8,128)(2,1)} %param.15) | copy-start | bytes 3145732
  379.6 118.5 %reduce-scatter.11.cloned.1.call-start = ((), (), s32[]{:S(2)}) async-start(), calls=%async_computation.10 | async-start | bytes 1572864 | tf_op jit(solution)/shard_map/reduce_scatter | solution.py:256
  448.0 6.9 %copy-start.31 = (bf16[512,512]{1,0:T(8,128)(2,1)S(1)}, bf16[512,512]{1,0:T(8,128)(2,1)}, u32[]{:S(2)}) copy-start(bf16[512,512]{1,0:T(8,128)(2,1)} %convert_element_type.182) | copy-start | bytes 1572868
  448.1 170.6 %all-reduce.6.cloned.1.call-start = ((), (), s32[]{:S(2)}) async-start(), calls=%async_computation.12 | async-start | bytes 8912896 | tf_op jit(solution)/shard_map/psum | solution.py:267
  479.1 19.0 %copy-start.6 = (bf16[1,256,1024]{2,1,0:T(8,128)(2,1)S(1)}, bf16[1,256,1024]{2,1,0:T(8,128)(2,1)}, u32[]{:S(2)}) copy-start(bf16[1,256,1024]{2,1,0:T(8,128)(2,1)} %param.10) | copy-start | bytes 1572868
  479.1 19.0 %copy-start.42 = (f32[1024]{0:T(1024)S(1)}, f32[1024]{0:T(1024)}, u32[]{:S(2)}) copy-start(f32[1024]{0:T(1024)} %param.12) | copy-start | bytes 12292
  479.1 20.5 %copy-start.50 = (f32[256]{0:T(256)S(1)}, f32[256]{0:T(256)}, u32[]{:S(2)}) copy-start(f32[256]{0:T(256)} %copy-done.49) | copy-start | bytes 3076
  479.1 20.5 %copy-start.48 = (f32[256]{0:T(256)S(1)}, f32[256]{0:T(256)}, u32[]{:S(2)}) copy-start(f32[256]{0:T(256)} %copy-done.47) | copy-start | bytes 3076
  481.6 19.6 %copy-start.44 = (f32[1024]{0:T(1024)S(1)}, f32[1024]{0:T(1024)}, u32[]{:S(2)}) copy-start(f32[1024]{0:T(1024)} %get-tuple-element.9) | copy-start | bytes 12292
  481.6 60.6 %copy-start.16 = (f32[256,1024]{1,0:T(8,128)S(1)}, f32[256,1024]{1,0:T(8,128)}, u32[]{:S(2)}) copy-start(f32[256,1024]{1,0:T(8,128)} %copy-done.15) | copy-start | bytes 3145732
  481.6 60.6 %copy-start.21 = (bf16[1,256,1024]{2,1,0:T(8,128)(2,1)S(1)}, bf16[1,256,1024]{2,1,0:T(8,128)(2,1)}, u32[]{:S(2)}) copy-start(bf16[1,256,1024]{2,1,0:T(8,128)(2,1)} %param.19) | copy-start | bytes 1572868
  498.1 44.1 %copy-start.19 = (bf16[256,1024]{1,0:T(8,128)(2,1)S(1)}, bf16[256,1024]{1,0:T(8,128)(2,1)}, u32[]{:S(2)}) copy-start(bf16[256,1024]{1,0:T(8,128)(2,1)} %reduce-scatter.11.cloned.1.call-done) | copy-start | bytes 1572868
  618.6 4.7 copy-start.29
  (37 other events, 99.1 us)
Sparse Core Ops, SparseCore 0:
  12.2 23.9 all-gather.5
  101.8 31.8 reduce-scatter.4
  137.4 45.9 all-gather.7
  184.8 44.6 all-gather.11
  243.3 75.4 reduce-scatter.8
  321.0 44.3 reduce-scatter.6
  369.3 20.5 all-gather.9
  393.6 81.1 all-reduce.7
  477.7 20.3 reduce-scatter.10
  503.0 115.6 all-reduce.5
where the time goes:
time: 643 us; the launch traced here: 634 us
  waiting for transfers between devices  362 us (56%)
  matrix products  99.2 us (15%)
  local copies, waits for them, and re-layouts  68.5 us (11%)
  other arithmetic  46.2 us (7%)
  blocking collectives  40.9 us (6%)
  between operations  16 us (2%)
    psum x1, waiting for transfers between devices, per_device(): lax.psum(grad_qkv.astype(jnp.bfloat16), ('dp', 'hidden'))  75 us
    reduce_scatter x1, waiting for transfers between devices, per_device(): lax.psum_scatter(jnp.einsum('nf,df->nd', piece, w_up, preferred_element_t...  67.2 us
    all_gather x1, waiting for transfers between devices, per_device(): second_rows = lax.all_gather(second_low, 'hidden', axis=0, tiled=True)  45 us
    reduce_scatter x1, waiting for transfers between devices, per_device(): lax.psum_scatter(jnp.dot(active, w_down, preferred_element_type=jnp.float...  43.8 us
    psum x1, blocking collectives, per_device(): lax.psum((grad_norm_first, grad_norm_second), ('dp', 'head', 'hidden'))  40.9 us
    all_gather x1, waiting for transfers between devices, per_device(): cot_rows = lax.all_gather(cot_low, 'hidden', axis=0, tiled=True)  40.3 us
    reduce_scatter x1, waiting for transfers between devices, per_device(): lax.psum_scatter(jnp.dot(mixed_low, w_out, preferred_element_type=jnp.flo...  31.9 us
    concatenate x8, local copies, waits for them, and re-layouts, hedgehog_map(): jnp.concatenate([jax.nn.softmax(logits, axis=-1), jax.nn.softmax(-logits,...  21.2 us
  transfers between devices with their start and end apart: 10, of which 10 were waited for; matrix products, arithmetic and copies ran while one was open for 17% of the time, Pallas kernels for 0%

commit v1 on v0

v1 whole, which is shorter than its diff:
```python
import jax, jax.numpy as jnp
from jax import lax
from jax.experimental import pallas as pl
from jax.experimental.pallas import tpu as pltpu
from jax.sharding import PartitionSpec as P
BF=jnp.bfloat16; F32=jnp.float32
NT=(((1,),(1,)),((),()))
TN=(((0,),(0,)),((),()))
SB=256

def mm(a,b): return jnp.dot(a,b,preferred_element_type=F32)
def mm_nt(a,b): return lax.dot_general(a,b,NT,preferred_element_type=F32)
def mm_tn(a,b): return lax.dot_general(a,b,TN,preferred_element_type=F32)

def half_ones(width, size):
    r=lax.broadcasted_iota(jnp.int32,(width,width),0)//size
    c=lax.broadcasted_iota(jnp.int32,(width,width),1)//size
    return (r==c).astype(F32).astype(BF)

def first_half(shape, size):
    return lax.broadcasted_iota(jnp.int32,shape,1)%(2*size) < size

def half_sum(t, ones):
    hi=t.astype(BF); lo=(t-hi.astype(F32)).astype(BF)
    return mm(hi,ones)+mm(lo,ones)

def features(x, w2, ones, size):
    u=mm(x,w2)
    h0=first_half(u.shape,size)
    big=jnp.float32(3e38)
    def both(f, fill):
        return jnp.where(h0, f(jnp.where(h0,u,fill)), f(jnp.where(h0,fill,u)))
    top=both(lambda t: jnp.max(t,axis=1,keepdims=True), -big)
    low=both(lambda t: jnp.min(t,axis=1,keepdims=True), big)
    e=jnp.concatenate([jnp.exp(u-top),jnp.exp(low-u)],axis=1)
    s=mm(e.astype(BF),ones)
    return e/s

def halves(t, h0):
    z=jnp.zeros_like(t)
    return jnp.where(h0,t,z), jnp.where(h0,z,t)

def attend(fq, fk, v, size):
    n=fq.shape[0]
    h0=first_half(fq.shape,size)
    fqs=halves(fq,h0)
    hv=first_half(v.shape,size)
    one=jnp.ones(v.shape,BF)
    ve=halves(jnp.concatenate([v,one],axis=1),h0)
    outs=[]
    for r in range(0,n,SB):
        ext=r+SB
        keep=(lax.broadcasted_iota(jnp.int32,(SB,ext),0)+r)>=lax.broadcasted_iota(jnp.int32,(SB,ext),1)
        acc=None
        for s in range(2):
            sc=mm_nt(fqs[s][r:r+SB],fk[:ext])
            sc=jnp.where(keep,sc,0.0).astype(BF)
            t=mm(sc,ve[s][:ext])
            acc=t if acc is None else acc+t
        outs.append(acc)
    p=jnp.concatenate(outs,axis=0)
    w=v.shape[1]
    rden=1.0/p[:,w:]
    return p[:,:w]*rden, rden

def attend_back(fq,fk,v,mixed,rden,datt,ones,size):
    n,w=v.shape
    wide=(n,2*w)
    h0=first_half(wide,size)
    dn=(datt*rden).astype(BF)
    dd=-half_sum(datt*mixed.astype(F32),ones)*rden
    hi=dd.astype(BF); lo=(dd-hi.astype(F32)).astype(BF)
    lane=lax.broadcasted_iota(jnp.int32,(n,w),1)%size
    zero=jnp.zeros((n,w),BF)
    ext_=jnp.where(lane==0,hi,jnp.where(lane==1,lo,zero))
    nx=halves(jnp.concatenate([dn,ext_],axis=1),h0)
    vx=jnp.concatenate([v,jnp.ones((n,w),BF)],axis=1)
    fqs=halves(fq,h0); fks=halves(fk,h0)
    dfq=[];dfk=[];dv=[]
    for r in range(0,n,SB):
        ext=r+SB
        keep=(lax.broadcasted_iota(jnp.int32,(SB,ext),0)+r)>=lax.broadcasted_iota(jnp.int32,(SB,ext),1)
        acc=0.0
        for s in range(2):
            ds=jnp.where(keep,mm_nt(nx[s][r:r+SB],vx[:ext]),0.0).astype(BF)
            acc=acc+mm(ds,fks[s][:ext])
        dfq.append(acc)
        left=n-r
        keep=lax.broadcasted_iota(jnp.int32,(SB,left),0)<=lax.broadcasted_iota(jnp.int32,(SB,left),1)
        ak=0.0; av=0.0
        for s in range(2):
            ds=jnp.where(keep,mm_nt(vx[r:r+SB],nx[s][r:]),0.0).astype(BF)
            ak=ak+mm(ds,fqs[s][r:])
            sc=jnp.where(keep,mm_nt(fk[r:r+SB],fqs[s][r:]),0.0).astype(BF)
            av=av+mm(sc,nx[s][r:,:w])
        dfk.append(ak); dv.append(av)
    cat=lambda t: jnp.concatenate(t,axis=0)
    return cat(dfq),cat(dfk),cat(dv)

def feature_back(f, df, ones):
    w=f.shape[1]//2
    f=f.astype(F32)
    part=f*(df-half_sum(f*df,ones))
    return (part[:,:w]-part[:,w:]).astype(BF)

def pair_weights(wf_ref, w2_ref):
    hd=wf_ref.shape[-1]
    w2_ref[...]=jnp.zeros_like(w2_ref)
    for t in range(2):
        for p in range(w2_ref.shape[1]):
            w2_ref[t,p,:hd,:hd]=wf_ref[t,2*p]
            w2_ref[t,p,hd:,hd:]=wf_ref[t,2*p+1]

def fwd_kernel(len_ref, rows_ref, wqkv_ref, wf_ref, wout_ref, proj_ref, feat_ref, mixed_ref, rden_ref, branch_ref, w2_ref):
    hd=wf_ref.shape[-1]; w=2*hd; n=rows_ref.shape[0]; pairs=w2_ref.shape[1]
    pair_weights(wf_ref,w2_ref)
    for i in range(3):
        proj_ref[i]=mm(rows_ref[...],wqkv_ref[i]).astype(BF)
    ones=half_ones(2*w,hd)
    valid=lax.broadcasted_iota(jnp.int32,(n,2*w),0)<len_ref[0,0]
    def body(p,_):
        c=pl.ds(pl.multiple_of(p*w,w),w)
        fq=features(proj_ref[0,:,c],w2_ref[0,p],ones,hd).astype(BF)
        fk=jnp.where(valid,features(proj_ref[1,:,c],w2_ref[1,p],ones,hd),0.0).astype(BF)
        feat_ref[0,p]=fq; feat_ref[1,p]=fk
        m,rd=attend(fq,fk,proj_ref[2,:,c],hd)
        mixed_ref[:,c]=m.astype(BF); rden_ref[:,c]=rd
        return 0
    lax.fori_loop(0,pairs,body,0)
    branch_ref[...]=mm(mixed_ref[...],wout_ref[...]).astype(branch_ref.dtype)

def bwd_kernel(rows_ref,wqkv_ref,wf_ref,wout_ref,proj_ref,feat_ref,mixed_ref,rden_ref,dbr_ref,
               gq_ref,gf_ref,go_ref,dfirst_ref,w2_ref,datt_ref,dproj_ref):
    hd=wf_ref.shape[-1]; w=2*hd; n=rows_ref.shape[0]; pairs=w2_ref.shape[1]
    pair_weights(wf_ref,w2_ref)
    ones=half_ones(2*w,hd); ones1=half_ones(w,hd)
    datt_ref[...]=mm_nt(dbr_ref[...],wout_ref[...])
    go_ref[...]=mm_tn(mixed_ref[...],dbr_ref[...]).astype(go_ref.dtype)
    def body(p,_):
        c=pl.ds(pl.multiple_of(p*w,w),w)
        fq=feat_ref[0,p]; fk=feat_ref[1,p]
        dfq,dfk,dv=attend_back(fq,fk,proj_ref[2,:,c],mixed_ref[:,c],rden_ref[:,c],datt_ref[:,c],ones1,hd)
        for t,(f,df) in enumerate(((fq,dfq),(fk,dfk))):
            du=feature_back(f,df,ones)
            g=mm_tn(proj_ref[t,:,c],du)
            gf_ref[t,2*p]=g[:hd,:hd].astype(gf_ref.dtype); gf_ref[t,2*p+1]=g[hd:,hd:].astype(gf_ref.dtype)
            dproj_ref[t,:,c]=mm_nt(du,w2_ref[t,p]).astype(BF)
        dproj_ref[2,:,c]=dv.astype(BF)
        return 0
    lax.fori_loop(0,pairs,body,0)
    acc=None
    for i in range(3):
        gq_ref[i]=mm_tn(rows_ref[...],dproj_ref[i]).astype(gq_ref.dtype)
        t=mm_nt(dproj_ref[i],wqkv_ref[i])
        acc=t if acc is None else acc+t
    dfirst_ref[...]=acc.astype(dfirst_ref.dtype)
VM=pl.BlockSpec(memory_space=pltpu.VMEM)
SM=pl.BlockSpec(memory_space=pltpu.SMEM)
S=jax.ShapeDtypeStruct
def fwd(length,rows,wqkv,wf,wout):
    n,d=rows.shape; c=wout.shape[0]; h=wf.shape[1]; hd=wf.shape[-1]
    return pl.pallas_call(fwd_kernel,
      out_shape=(S((3,n,c),BF),S((2,h//2,n,4*hd),BF),S((n,c),BF),S((n,c),F32),S((n,d),BF)),
      in_specs=[SM,VM,VM,VM,VM],out_specs=[VM]*5,
      scratch_shapes=[pltpu.VMEM((2,h//2,2*hd,2*hd),BF)],
      compiler_params=pltpu.CompilerParams(vmem_limit_bytes=56*2**20))(length,rows,wqkv,wf,wout)
def bwd(rows,wqkv,wf,wout,proj,feat,mixed,rden,dbr):
    n,d=rows.shape; c=wout.shape[0]; h=wf.shape[1]; hd=wf.shape[-1]
    return pl.pallas_call(bwd_kernel,
      out_shape=(S((3,d,c),BF),S((2,h,hd,hd),F32),S((c,d),BF),S((n,d),BF)),
      in_specs=[VM]*9,out_specs=[VM]*4,
      scratch_shapes=[pltpu.VMEM((2,h//2,2*hd,2*hd),BF),pltpu.VMEM((n,c),F32),pltpu.VMEM((3,n,c),BF)],
      compiler_params=pltpu.CompilerParams(vmem_limit_bytes=56*2**20))(rows,wqkv,wf,wout,proj,feat,mixed,rden,dbr)

EPS=1e-05

def normalize(values, gain):
    average = jnp.mean(values, axis=-1, keepdims=True)
    centred = values - average
    spread = jnp.mean(centred * centred, axis=-1, keepdims=True)
    return centred * lax.rsqrt(spread + EPS) * gain

def smooth_gate(values):
    return jax.nn.gelu(values, approximate=True)

def per_device(
    tokens, lengths, norm_first, w_qkv, w_feature, w_out, norm_second, w_up, w_down, cotangent
):
    wqkv=jnp.transpose(w_qkv,(1,0,2))
    residual_in = tokens[0].astype(jnp.float32)
    normed_first, first_back = jax.vjp(normalize, residual_in, norm_first)
    first_low = normed_first.astype(jnp.bfloat16)
    first_rows = lax.all_gather(first_low, "head", axis=0, tiled=True)
    cot_low = cotangent[0]
    cot_rows = lax.all_gather(cot_low, "hidden", axis=0, tiled=True)
    proj,feat,mixed,rden,part=fwd(lengths,first_rows,wqkv,w_feature,w_out)
    branch = lax.psum_scatter(part, "head", scatter_dimension=0, tiled=True).astype(jnp.float32)
    middle = residual_in + branch
    normed_second, second_back = jax.vjp(normalize, middle, norm_second)
    second_low = normed_second.astype(jnp.bfloat16)
    second_rows = lax.all_gather(second_low, "hidden", axis=0, tiled=True)
    hidden_pre = jnp.dot(second_rows, w_up, preferred_element_type=jnp.float32)
    active = smooth_gate(hidden_pre).astype(jnp.bfloat16)
    gate_grad = jax.vjp(smooth_gate, hidden_pre)[1]
    d_active = jnp.einsum("nd,fd->nf", cot_rows, w_down, preferred_element_type=jnp.float32)
    d_pre = gate_grad(d_active)[0].astype(jnp.bfloat16)
    d_second = lax.psum_scatter(
        jnp.einsum("nf,df->nd", d_pre, w_up, preferred_element_type=jnp.float32).astype(jnp.bfloat16),
        "hidden",
        scatter_dimension=0,
        tiled=True,
    ).astype(jnp.float32)
    mlp_result = lax.psum_scatter(
        jnp.dot(active, w_down, preferred_element_type=jnp.float32).astype(jnp.bfloat16),
        "hidden",
        scatter_dimension=0,
        tiled=True,
    ).astype(jnp.float32)
    block_out = (middle + mlp_result).astype(jnp.bfloat16)
    grad_down = jnp.einsum("nf,nd->fd", active, cot_rows, preferred_element_type=jnp.float32)
    grad_up = jnp.einsum("nd,nf->df", second_rows, d_pre, preferred_element_type=jnp.float32)
    d_middle_norm, grad_norm_second = second_back(d_second)
    d_middle = cot_low.astype(jnp.float32) + d_middle_norm
    d_branch_rows = lax.all_gather(d_middle.astype(jnp.bfloat16), "head", axis=0, tiled=True)
    gq,grad_feature,go,dfirst=bwd(first_rows,wqkv,w_feature,w_out,proj,feat,mixed,rden,d_branch_rows)
    d_first = lax.psum_scatter(dfirst, "head", scatter_dimension=0, tiled=True).astype(jnp.float32)
    d_input_norm, grad_norm_first = first_back(d_first)
    grad_tokens = d_middle + d_input_norm
    grad_up, grad_down = (
        lax.psum(grad_up.astype(jnp.bfloat16), ("dp", "head")).astype(jnp.float32),
        lax.psum(grad_down.astype(jnp.bfloat16), ("dp", "head")).astype(jnp.float32),
    )
    gq, grad_feature, go = (
        lax.psum(gq, ("dp", "hidden")).astype(jnp.float32),
        lax.psum(grad_feature.astype(jnp.bfloat16), ("dp", "hidden")).astype(jnp.float32),
        lax.psum(go, ("dp", "hidden")).astype(jnp.float32),
    )
    grad_norm_first, grad_norm_second = lax.psum(
        (grad_norm_first, grad_norm_second), ("dp", "head", "hidden")
    )
    return (
        block_out[None],
        grad_tokens[None],
        grad_norm_first,
        jnp.transpose(gq,(1,0,2)),
        grad_feature,
        go,
        grad_norm_second,
        grad_up,
        grad_down,
    )


def solution(mesh):
    in_specs = (
        P(("dp", "hidden"), "head", None),
        P(("dp", "hidden"), None),
        P(),
        P(None, None, "head"),
        P(None, "head", None, None),
        P("head", None),
        P(),
        P(None, "hidden"),
        P("hidden", None),
        P(("dp", "hidden"), "head", None),
    )
    out_specs = (
        P(("dp", "hidden"), "head", None),
        P(("dp", "hidden"), "head", None),
        P(),
        P(None, None, "head"),
        P(None, "head", None, None),
        P("head", None),
        P(),
        P(None, "hidden"),
        P("hidden", None),
    )
    return jax.shard_map(
        per_device, mesh=mesh, in_specs=in_specs, out_specs=out_specs, check_vma=False
    )
```

time: 643 us -> 538 us (0.84); the launches traced: 634 us -> 537 us
  local copies, waits for them, and re-layouts: 68.5 us -> 1.45 us
  matrix products: 99.2 us -> 34.6 us
  Pallas kernels: 0 us -> 35.2 us
  waiting for transfers between devices: 362 us -> 372 us
  other arithmetic: 46.2 us -> 37 us
    dot_general x29 -> x1, matrix products: 58.4 us -> 3.69 us  [per_device(): jnp.einsum('nf,df->nd', d_pre, w_up, preferred_element_type=jnp.float32)]
    psum x1, waiting for transfers between devices: 12.9 us -> 61.2 us  [per_device(): lax.psum(grad_up.astype(jnp.bfloat16), ('dp', 'head')).astype(jnp.float32)]
    reduce_scatter x3, waiting for transfers between devices: 116 us -> 72.1 us  [the longest x1 35.7 us: per_device(): lax.psum_scatter(jnp.einsum('nf,df->nd', d_pre, w_up, preferred_element_t...]
    pallas_call x0 -> x2, Pallas kernels: none -> 35.2 us  [the longest x1 22.7 us: bwd(): pl.pallas_call(bwd_kernel, out_shape=(S((3, d, c), BF), S((2, h, hd, hd),...]
    concatenate x8 -> x0, local copies, waits for them, and re-layouts: 21.2 us -> none  [hedgehog_map(): jnp.concatenate([jax.nn.softmax(logits, axis=-1), jax.nn.softmax(-logits,...]
    unnamed x121 -> x24, local copies, waits for them, and re-layouts: 18.9 us -> 1.45 us
    div x4 -> x0, matrix products: 10.6 us -> none  [the longest x2 5.37 us: hedgehog_map(): jax.nn.softmax(-logits, axis=-1)]
    convert_element_type x4 -> x0, local copies, waits for them, and re-layouts: 7.66 us -> none  [the longest x2 4.94 us: mixed_of(): (numer / denom[..., None]).reshape(row_count, -1).astype(jnp.bfloat16)]
  transfers between devices with their start and end apart: 10 -> 10, of which waited for: 10 -> 10; matrix products, arithmetic and copies ran while one was open for 17% -> 7% of each run, Pallas kernels for 0% -> 4%
where the time goes in v1:
time: 538 us; the launch traced here: 537 us
  waiting for transfers between devices  372 us (69%)
  blocking collectives  41 us (8%)
  other arithmetic  37 us (7%)
  Pallas kernels  35.2 us (7%)
  matrix products  34.6 us (6%)
  between operations  14.9 us (3%)
    psum x1, waiting for transfers between devices, per_device(): lax.psum(gq, ('dp', 'hidden')).astype(jnp.float32)  74.1 us
    psum x1, waiting for transfers between devices, per_device(): lax.psum(grad_up.astype(jnp.bfloat16), ('dp', 'head')).astype(jnp.float32)  61.2 us
    all_gather x1, waiting for transfers between devices, per_device(): second_rows = lax.all_gather(second_low, 'hidden', axis=0, tiled=True)  45.3 us
    reduce_scatter x1, waiting for transfers between devices, per_device(): lax.psum_scatter(jnp.dot(active, w_down, preferred_element_type=jnp.float...  44.4 us
    psum x1, blocking collectives, per_device(): lax.psum((grad_norm_first, grad_norm_second), ('dp', 'head', 'hidden'))  41 us
    all_gather x1, waiting for transfers between devices, per_device(): cot_rows = lax.all_gather(cot_low, 'hidden', axis=0, tiled=True)  40.3 us
    reduce_scatter x1, waiting for transfers between devices, per_device(): lax.psum_scatter(jnp.einsum('nf,df->nd', d_pre, w_up, preferred_element_t...  35.7 us
    all_gather x1, waiting for transfers between devices, per_device(): first_rows = lax.all_gather(first_low, 'head', axis=0, tiled=True)  23.5 us
  transfers between devices with their start and end apart: 10, of which 10 were waited for; matrix products, arithmetic and copies ran while one was open for 7% of the time, Pallas kernels for 4%

profile of v1, /device:TPU:0, one launch (start us, length us, event | category | flops | bytes accessed | tf_op | source)
XLA Modules:
  0.0 536.8 jit_solution(5656570753511733789)
XLA Ops:
  9.9 2.2 fusion.26
  12.8 23.5 %all-gather.6.cloned.1.call-done.rows_ref = bf16[512,1024]{1,0:T(8,128)(2,1)} async-done(((bf16[256,1024]{1,0:T(8,128)(2,1)}), bf16[512,1024]{1,0:T(8,128)(2,1)}) %all-gather.6.cloned.1.call-update) | async-done | bytes 1048592 | tf_op jit(solution)/shard_map/all_gather | solution.py:193
  36.3 12.5 %shard_map.169 = (bf16[3,512,512]{2,1,0:T(8,128)(2,1)}, bf16[2,4,512,256]{3,2,1,0:T(8,128)(2,1)}, bf16[512,512]{1,0:T(8,128)(2,1)}, f32[512,512]{1,0:T(8,128)}, bf16[512,1024]{1,0:T(8,128)(2,1)}) custom-call(s32[1,1]{1,0:T(1,128)S(6)} %copy.24.len_ref, bf16[512,1024]{1,0:T(8,128)(2,1)} %all-gather.6.cloned.1.call-done.rows_ref, ...), custom_call_target="tpu_custom_call" | custom-call | tf_op jit(solution)/shard_map/pallas_call | solution.py:162
  48.9 20.4 %reduce-scatter.5.cloned.1.call-done = bf16[256,1024]{1,0:T(8,128)(2,1)} async-done(((bf16[512,1024]{1,0:T(8,128)(2,1)}), bf16[256,1024]{1,0:T(8,128)(2,1)}) %reduce-scatter.5.cloned.1.call-update) | async-done | bytes 524304 | tf_op jit(solution)/shard_map/reduce_scatter | solution.py:197
  72.0 2.1 multiply_convert_fusion.1
  74.9 45.3 %all-gather.8.cloned.1.call-done = bf16[1024,1024]{1,0:T(8,128)(2,1)} async-done(((bf16[256,1024]{1,0:T(8,128)(2,1)}), bf16[1024,1024]{1,0:T(8,128)(2,1)}) %all-gather.8.cloned.1.call-update) | async-done | bytes 2097168 | tf_op jit(solution)/shard_map/all_gather | solution.py:201
  120.2 5.9 %fusion.40 = f32[1024,1024]{1,0:T(8,128)} fusion(bf16[1024,1024]{1,0:T(8,128)(2,1)} %all-gather.8.cloned.1.call-done, bf16[1024,1024]{1,0:T(8,128)(2,1)S(1)} %copy-done), kind=kOutput, calls=%fused_computation.63 | convolution fusion | flops 2147483648 | bytes 8388608 | tf_op jit(solution)/shard_map/dot_general | solution.py:202
  126.1 40.3 %all-gather.12.cloned.1.call-done = bf16[1,1024,1024]{2,1,0:T(8,128)(2,1)} async-done(((bf16[1,256,1024]{2,1,0:T(8,128)(2,1)}), bf16[1,1024,1024]{2,1,0:T(8,128)(2,1)}) %all-gather.12.cloned.1.call-update) | async-done | bytes 2097168 | tf_op jit(solution)/shard_map/all_gather | solution.py:195
  166.3 7.9 %fusion.6 = bf16[1024,1024]{1,0:T(8,128)(2,1)S(1)} fusion(f32[1024,1024]{1,0:T(8,128)} %fusion.40, bf16[1024,1024]{1,0:T(8,128)(2,1)} %param.18, bf16[1,1024,1024]{2,1,0:T(8,128)(2,1)} %all-gather.12.cloned.1.call-done), kind=kOutput, calls=%fused_computation.8 | convolution fusion | flops 2168455168 | bytes 10485760 | tf_op jit(solution)/shard_map/nd,fd->nf/dot_general | solution.py:205
  174.3 1.4 copy-done.11
  175.7 3.7 convolution_convert_fusion.1
  179.5 6.9 %convolution_convert_fusion.2 = bf16[1024,1024]{1,0:T(8,128)(2,1)} fusion(bf16[1024,1024]{1,0:T(8,128)(2,1)} %param.18, f32[1024,1024]{1,0:T(8,128)} %fusion.40), kind=kOutput, calls=%fused_computation.17 | convolution fusion | flops 2157969408 | bytes 8388608 | tf_op jit(solution)/shard_map/dot_general | solution.py:214
  186.4 35.7 %reduce-scatter.9.cloned.1.call-done = bf16[256,1024]{1,0:T(8,128)(2,1)} async-done(((bf16[1024,1024]{1,0:T(8,128)(2,1)}), bf16[256,1024]{1,0:T(8,128)(2,1)}) %reduce-scatter.9.cloned.1.call-update) | async-done | bytes 524304 | tf_op jit(solution)/shard_map/reduce_scatter | solution.py:207
  222.2 1.6 fusion.30
  223.7 44.4 %reduce-scatter.7.cloned.1.call-done = bf16[256,1024]{1,0:T(8,128)(2,1)} async-done(((bf16[1024,1024]{1,0:T(8,128)(2,1)}), bf16[256,1024]{1,0:T(8,128)(2,1)}) %reduce-scatter.7.cloned.1.call-update) | async-done | bytes 524304 | tf_op jit(solution)/shard_map/reduce_scatter | solution.py:213
  268.1 2.5 fusion.39
  271.9 6.1 %convolution_convert_fusion = bf16[1024,1024]{1,0:T(8,128)(2,1)} fusion(bf16[1024,1024]{1,0:T(8,128)(2,1)} %all-gather.8.cloned.1.call-done, bf16[1024,1024]{1,0:T(8,128)(2,1)} %copy-done.11), kind=kOutput, calls=%fused_computation.15 | convolution fusion | flops 2148532224 | bytes 6291456 | tf_op jit(solution)/shard_map/nd,nf->df/dot_general | solution.py:221
  277.9 4.1 fusion.13
  282.1 10.2 %all-gather.10.cloned.1.call-done.dbr_ref = bf16[512,1024]{1,0:T(8,128)(2,1)} async-done(((bf16[256,1024]{1,0:T(8,128)(2,1)}), bf16[512,1024]{1,0:T(8,128)(2,1)}) %all-gather.10.cloned.1.call-update) | async-done | bytes 1048592 | tf_op jit(solution)/shard_map/all_gather | solution.py:224
  292.3 22.7 %shard_map.170 = (bf16[3,1024,512]{2,1,0:T(8,128)(2,1)}, f32[2,8,64,64]{3,2,1,0:T(8,128)}, bf16[512,1024]{1,0:T(8,128)(2,1)}, bf16[512,1024]{1,0:T(8,128)(2,1)}) custom-call(bf16[512,1024]{1,0:T(8,128)(2,1)} %all-gather.6.cloned.1.call-done.rows_ref, bf16[3,1024,512]{2,1,0:T(8,128)(2,1)} %bitcast.79, bf16[2,8,64,64]{3,2,1,0:T(8,128)(2,1)} %wf_ref.3, ...), custom_call_target="tpu_custom_call" | custom-call | tf_op jit(solution)/shard_map/pallas_call | solution.py:169
  315.4 1.8 convert_element_type.82
  317.2 61.2 %all-reduce.8.cloned.1.call-done = (bf16[1024,1024]{1,0:T(8,128)(2,1)}, bf16[1024,1024]{1,0:T(8,128)(2,1)}) async-done(((bf16[1024,1024]{1,0:T(8,128)(2,1)}, bf16[1024,1024]{1,0:T(8,128)(2,1)}), (bf16[1024,1024]{1,0:T(8,128)(2,1)}, bf16[1024,1024]{1,0:T(8,128)(2,1)})) %all-reduce.8.cloned.1.call-update) | async-done | bytes 4194320 | tf_op jit(solution)/shard_map/psum | solution.py:230
  378.4 4.2 convert_element_type.86
  382.6 2.5 convert_element_type.88
  385.1 16.0 %reduce-scatter.11.cloned.1.call-done = bf16[256,1024]{1,0:T(8,128)(2,1)} async-done(((bf16[512,1024]{1,0:T(8,128)(2,1)}), bf16[256,1024]{1,0:T(8,128)(2,1)}) %reduce-scatter.11.cloned.1.call-update) | async-done | bytes 524304 | tf_op jit(solution)/shard_map/reduce_scatter | solution.py:226
  402.4 1.6 fusion.31
  404.1 41.0 %all-reduce = (f32[1024]{0:T(1024)}, f32[1024]{0:T(1024)}) all-reduce(f32[1024]{0:T(1024)S(1)} %get-tuple-element.29, f32[1024]{0:T(1024)S(1)} %get-tuple-element.27), channel_id=1, replica_groups=mesh['dp'=4,'head'=2,'hidden'=4] {'dp','head','hidden'}, use_global_device_ids=true, to_apply=%region_13.0 | all-reduce | flops 2048 | bytes 16384 | tf_op jit(solution)/shard_map/psum | solution.py:238
  445.1 2.5 add_bitcast_fusion
  447.6 74.1 %all-reduce.6.cloned.1.call-done = (bf16[1024,3,512]{2,0,1:T(8,128)(2,1)}, bf16[2,8,64,64]{3,2,1,0:T(8,128)(2,1)}, bf16[512,1024]{1,0:T(8,128)(2,1)}) async-done(((bf16[1024,3,512]{2,0,1:T(8,128)(2,1)}, bf16[2,8,64,64]{3,2,1,0:T(8,128)(2,1)}, bf16[512,1024]{1,0:T(8,128)(2,1)}), (bf16[1024,3,512]{2,0,1:T(8,128)(2,1)}, bf16[2,8,64,64]{3,2,1,0:T(8,128)(2,1)}, ...) | async-done | bytes 4325392 | tf_op jit(solution)/shard_map/psum | solution.py:234
  521.6 1.9 convert_element_type.83
  523.6 2.8 convert_element_type.84
  526.4 3.6 transpose.17
  (57 shorter events, 9.5 us)
Async XLA Ops:
  7.2 113.0 %copy-start = (bf16[1024,1024]{1,0:T(8,128)(2,1)S(1)}, bf16[1024,1024]{1,0:T(8,128)(2,1)}, u32[]{:S(2)}) copy-start(bf16[1024,1024]{1,0:T(8,128)(2,1)} %param.17) | copy-start | bytes 6291460
  7.2 29.1 %all-gather.6.cloned.1.call-start = ((), (), s32[]{:S(2)}) async-start(), calls=%async_computation.4 | async-start | bytes 1572864 | tf_op jit(solution)/shard_map/all_gather | solution.py:193
  9.9 59.4 %copy-start.2 = (bf16[1,256,1024]{2,1,0:T(8,128)(2,1)S(1)}, bf16[1,256,1024]{2,1,0:T(8,128)(2,1)}, u32[]{:S(2)}) copy-start(bf16[1,256,1024]{2,1,0:T(8,128)(2,1)} %param.10) | copy-start | bytes 1572868
  12.1 57.2 %reduce-scatter.5.cloned.1.call-start = ((), (), s32[]{:S(2)}) async-start(), calls=%async_computation.5 | async-start | bytes 1572864 | tf_op jit(solution)/shard_map/reduce_scatter | solution.py:197
  36.3 35.6 %copy-start.8 = (f32[1024]{0:T(1024)S(1)}, f32[1024]{0:T(1024)}, u32[]{:S(2)}) copy-start(f32[1024]{0:T(1024)} %param.16) | copy-start | bytes 12292
  48.9 71.3 %all-gather.8.cloned.1.call-start = ((), (), s32[]{:S(2)}) async-start(), calls=%async_computation.6 | async-start | bytes 2621440 | tf_op jit(solution)/shard_map/all_gather | solution.py:201
  74.1 92.3 %all-gather.12.cloned.1.call-start = ((), (), s32[]{:S(2)}) async-start(), calls=%async_computation.11 | async-start | bytes 2621440 | tf_op jit(solution)/shard_map/all_gather | solution.py:195
  74.6 147.5 %reduce-scatter.9.cloned.1.call-start = ((), (), s32[]{:S(2)}) async-start(), calls=%async_computation.8 | async-start | bytes 2621440 | tf_op jit(solution)/shard_map/reduce_scatter | solution.py:207
  174.3 1.4 copy-start.11
  179.4 42.7 %copy-start.3 = (bf16[256,1024]{1,0:T(8,128)(2,1)S(1)}, bf16[256,1024]{1,0:T(8,128)(2,1)}, u32[]{:S(2)}) copy-start(bf16[256,1024]{1,0:T(8,128)(2,1)} %reduce-scatter.5.cloned.1.call-done) | copy-start | bytes 1572868
  179.4 88.7 %reduce-scatter.7.cloned.1.call-start = ((), (), s32[]{:S(2)}) async-start(), calls=%async_computation.7 | async-start | bytes 2621440 | tf_op jit(solution)/shard_map/reduce_scatter | solution.py:213
  186.3 84.2 %copy-start.4 = (bf16[1,256,1024]{2,1,0:T(8,128)(2,1)S(1)}, bf16[1,256,1024]{2,1,0:T(8,128)(2,1)}, u32[]{:S(2)}) copy-start(bf16[1,256,1024]{2,1,0:T(8,128)(2,1)} %param.19) | copy-start | bytes 1572868
  186.4 106.0 %all-gather.10.cloned.1.call-start = ((), (), s32[]{:S(2)}) async-start(), calls=%async_computation.9 | async-start | bytes 1572864 | tf_op jit(solution)/shard_map/all_gather | solution.py:224
  271.6 106.8 %all-reduce.8.cloned.1.call-start = ((), (), s32[]{:S(2)}) async-start(), calls=%async_computation.13 | async-start | bytes 8388608 | tf_op jit(solution)/shard_map/psum | solution.py:230
  271.8 6.1 %copy-start.9 = (bf16[1,1024,1024]{2,1,0:T(8,128)(2,1)S(1)}, bf16[1,1024,1024]{2,1,0:T(8,128)(2,1)}, u32[]{:S(2)}) copy-start(bf16[1,1024,1024]{2,1,0:T(8,128)(2,1)} %all-gather.12.cloned.1.call-done) | copy-start | bytes 6291460
  271.9 6.1 %copy-start.10 = (f32[1024,1024]{1,0:T(8,128)S(1)}, f32[1024,1024]{1,0:T(8,128)}, u32[]{:S(2)}) copy-start(f32[1024,1024]{1,0:T(8,128)} %fusion.40) | copy-start | bytes 12582916
  282.1 119.0 %reduce-scatter.11.cloned.1.call-start = ((), (), s32[]{:S(2)}) async-start(), calls=%async_computation.10 | async-start | bytes 1572864 | tf_op jit(solution)/shard_map/reduce_scatter | solution.py:226
  315.1 206.6 %all-reduce.6.cloned.1.call-start = ((), (), s32[]{:S(2)}) async-start(), calls=%async_computation.12 | async-start | bytes 8912896 | tf_op jit(solution)/shard_map/psum | solution.py:234
  378.4 4.2 copy-start.6
  382.6 18.4 %copy-start.7 = (f32[1024]{0:T(1024)S(1)}, f32[1024]{0:T(1024)}, u32[]{:S(2)}) copy-start(f32[1024]{0:T(1024)} %param.12) | copy-start | bytes 12292
  521.6 4.7 copy-start.5
  526.4 3.6 copy-start.1
Sparse Core Ops, SparseCore 0:
  12.3 23.9 all-gather.5
  49.0 20.3 reduce-scatter.4
  74.2 45.9 all-gather.7
  121.7 44.6 all-gather.11
  179.5 42.5 reduce-scatter.8
  224.9 43.1 reduce-scatter.6
  271.7 20.6 all-gather.9
  297.2 81.1 all-reduce.7
  380.6 20.3 reduce-scatter.10
  406.0 115.6 all-reduce.5

commit v2 on v1

--- a/solution.py
+++ b/solution.py
@@ -251,6 +251,253 @@
     )
 
 
+MESH=pl.DeviceIdType.MESH
+ANY=pl.BlockSpec(memory_space=pl.ANY)
+EPS=1e-05
+
+def place():
+    dp=lax.axis_index("dp")
+    return dp//2, dp%2, lax.axis_index("head"), lax.axis_index("hidden")
+
+def around():
+    x,c,y,z=place()
+    return ((1-x)*2+c,y,z), (x*2+c,1-y,z), (x*2+1-c,y,z)
+
+def along(step):
+    x,c,y,z=place()
+    return (x*2+c,y,z+step)
+
+def remote(src,dst,sems,i,dev):
+    return pltpu.make_async_remote_copy(src_ref=src,dst_ref=dst,send_sem=sems.at[0,i],recv_sem=sems.at[1,i],device_id=dev,device_id_type=MESH)
+
+def greet(peers, line):
+    _,_,_,z=place()
+    last=lax.axis_size("hidden")-1
+    bar=pltpu.get_barrier_semaphore()
+    for d in peers:
+        pl.semaphore_signal(bar,inc=1,device_id=d,device_id_type=MESH)
+    count=len(peers)
+    if line:
+        for step in (1,-1):
+            @pl.when((z<last) if step==1 else (z>0))
+            def _():
+                pl.semaphore_signal(bar,inc=1,device_id=along(step),device_id_type=MESH)
+        count=count+jnp.where(z<last,1,0)+jnp.where(z>0,1,0)
+    pl.semaphore_wait(bar,count)
+
+def unit(values):
+    centred=values-jnp.mean(values,axis=-1,keepdims=True)
+    r=lax.rsqrt(jnp.mean(centred*centred,axis=-1,keepdims=True)+EPS)
+    return centred*r, r
+
+def k1_kernel(len_ref,tok,g1,wqkv,wf,wout,g2,wup,wdn,cot,
+              tok_o,rows_o,proj_o,feat_o,mixed_o,rden_o,mid_o,sec_o,wu_o,wd_o,cot_o,
+              T,rows,wq,wo,proj,feat,mixed,rden,own,snd,rcv,mid,sec,w2,loc,rem,zr,zl,dd):
+    x,c,y,z=place()
+    last=lax.axis_size("hidden")-1
+    nx,ny,nc=around()
+    R=tok.shape[0]; n=2*R; d=tok.shape[1]
+    hd=wf.shape[-1]; w=2*hd; pairs=w2.shape[1]
+    q=x*2+y
+    lc=lambda s,t,i: pltpu.make_async_copy(s,t,loc.at[i])
+    mine=pl.ds(pl.multiple_of(y*R,R),R); other=pl.ds(pl.multiple_of((1-y)*R,R),R)
+    fs=wup.shape[1]//4
+    cols=pl.ds(pl.multiple_of(q*fs,fs),fs)
+    hu=wup.shape[0]//2; hw=fs//2
+    uh=pl.ds(pl.multiple_of(c*hu,hu),hu); dh=pl.ds(pl.multiple_of(c*hw,hw),hw)
+    l_tok=lc(tok,T.at[mine],0); l_wq=[lc(wqkv.at[i],wq.at[i],1+i) for i in range(3)]; l_wo=lc(wout,wo,4)
+    l_wu=lc(wup.at[:,cols],wu_o.at[z],5); l_wd=lc(wdn.at[cols],wd_o.at[z],6); l_cot=lc(cot,cot_o.at[q],7)
+    l_tok.start()
+    for k in l_wq: k.start()
+    greet((nx,ny,nc),True)
+    r_tok=remote(tok,T.at[mine],rem,0,ny)
+    r_tok.start()
+    def z_copies(s,right):
+        j=(z-s+1) if right else (z+s-1)
+        sems,dev=(zr,along(1)) if right else (zl,along(-1))
+        if s==1:
+            su=wup.at[uh,cols]
+            sd=wdn.at[pl.ds(pl.multiple_of(q*fs+c*hw,hw),hw)]
+        else:
+            su=wu_o.at[j,uh]; sd=wd_o.at[j,dh]
+        return [remote(su,wu_o.at[j,uh],sems,2*(s-1),dev),remote(sd,wd_o.at[j,dh],sems,2*(s-1)+1,dev)]
+    def z_send(s):
+        for right in (True,False):
+            ok=((z<last)&(z-s+1>=0)) if right else ((z>0)&(z+s-1<=last))
+            @pl.when(ok)
+            def _():
+                for k in z_copies(s,right): k.start()
+    def z_recv(s):
+        for right in (True,False):
+            ok=(z-s>=0) if right else (z+s<=last)
+            j=(z-s) if right else (z+s)
+            @pl.when(ok)
+            def _():
+                jj=jnp.clip(j,0,last)
+                sems=zr if right else zl
+                remote(wu_o.at[jj,uh],wu_o.at[jj,uh],sems,2*(s-1),nc).wait_recv()
+                remote(wd_o.at[jj,dh],wd_o.at[jj,dh],sems,2*(s-1)+1,nc).wait_recv()
+                i=2*(s-1)+(0 if right else 2*last)
+                remote(wu_o.at[jj,uh],wu_o.at[jj,uh],dd,i,nc).start()
+                remote(wd_o.at[jj,dh],wd_o.at[jj,dh],dd,i+1,nc).start()
+    def z_end():
+        for s in range(1,last+1):
+            for right in (True,False):
+                ok=((z<last)&(z-s+1>=0)) if right else ((z>0)&(z+s-1<=last))
+                @pl.when(ok)
+                def _():
+                    for k in z_copies(s,right): k.wait_send()
+                got=(z-s>=0) if right else (z+s<=last)
+                j=(z-s) if right else (z+s)
+                @pl.when(got)
+                def _():
+                    jj=jnp.clip(j,0,last)
+                    i=2*(s-1)+(0 if right else 2*last)
+                    co=1-c
+                    ou=pl.ds(pl.multiple_of(co*hu,hu),hu); od=pl.ds(pl.multiple_of(co*hw,hw),hw)
+                    remote(wu_o.at[jj,uh],wu_o.at[jj,ou],dd,i,nc).wait()
+                    remote(wd_o.at[jj,dh],wd_o.at[jj,od],dd,i+1,nc).wait()
+    z_send(1)
+    r_cx=remote(cot,cot_o.at[q],rem,1,nx)
+    r_cx.start()
+    for k in (l_wo,l_wu,l_wd,l_cot): k.start()
+    pair_weights(wf,w2)
+    ones=half_ones(2*w,hd)
+    def first(at):
+        xh,_=unit(T[at].astype(F32))
+        rows[at]=(xh*g1[...]).astype(BF)
+    def project(at):
+        for i in range(3): proj[i,at]=mm(rows[at],wq[i]).astype(BF)
+    l_tok.wait()
+    first(mine)
+    for k in l_wq: k.wait()
+    project(mine)
+    r_tok.wait_recv()
+    r_cy=remote(cot,cot_o.at[q],rem,2,ny)
+    r_cy.start()
+    l_tok_o=lc(T,tok_o,8); l_tok_o.start()
+    first(other)
+    l_rows=lc(rows,rows_o,9); l_rows.start()
+    project(other)
+    l_proj=lc(proj,proj_o,10); l_proj.start()
+    valid=lax.broadcasted_iota(jnp.int32,(n,2*w),0)<len_ref[0,0]
+    def body(p,_):
+        cc=pl.ds(pl.multiple_of(p*w,w),w)
+        fq=features(proj[0,:,cc],w2[0,p],ones,hd).astype(BF)
+        fk=jnp.where(valid,features(proj[1,:,cc],w2[1,p],ones,hd),0.0).astype(BF)
+        feat[0,p]=fq; feat[1,p]=fk
+        m,rd=attend(fq,fk,proj[2,:,cc],hd)
+        mixed[:,cc]=m.astype(BF); rden[:,cc]=rd
+        return 0
+    lax.fori_loop(0,pairs//2,body,0)
+    z_recv(1)
+    z_send(2)
+    lax.fori_loop(pairs//2,pairs,body,0)
+    l_wo.wait()
+    snd[...]=mm(mixed[other],wo[...]).astype(BF)
+    r_part=remote(snd,rcv,rem,3,ny)
+    r_part.start()
+    own[...]=mm(mixed[mine],wo[...])
+    l_feat=lc(feat,feat_o,11); l_mixed=lc(mixed,mixed_o,12); l_rden=lc(rden,rden_o,13)
+    for k in (l_feat,l_mixed,l_rden): k.start()
+    z_recv(2)
+    z_send(3)
+    r_cy.wait_recv()
+    yq=x*2+1-y
+    r_cf=remote(cot_o.at[yq],cot_o.at[yq],rem,4,nx)
+    r_cf.start()
+    r_part.wait_recv()
+    middle=T[mine].astype(F32)+(own[...]+rcv[...].astype(F32))
+    mid[...]=middle
+    xh,_=unit(middle)
+    sec[...]=(xh*g2[...]).astype(BF)
+    l_mid=lc(mid,mid_o,14); l_sec=lc(sec,sec_o,15)
+    l_mid.start(); l_sec.start()
+    z_recv(3)
+    r_cx.wait_recv(); r_cf.wait_recv()
+    for k in (r_tok,r_cx,r_cy,r_part,r_cf): k.wait_send()
+    z_end()
+    for k in (l_wu,l_wd,l_cot,l_tok_o,l_rows,l_proj,l_feat,l_mixed,l_rden,l_mid,l_sec): k.wait()
+
+def k1(length,tok,g1,wqkv,wf,wout,g2,wup,wdn,cot):
+    R,d=tok.shape; n=2*R; c=wout.shape[0]; h=wf.shape[1]; hd=wf.shape[-1]; f=wup.shape[1]
+    last=lax.axis_size("hidden")-1
+    big=[S((n,d),BF),S((n,d),BF),S((3,n,c),BF),S((2,h//2,n,4*hd),BF),S((n,c),BF),S((n,c),F32),S((R,d),F32),S((R,d),BF)]
+    vm=[pltpu.VMEM(s.shape,s.dtype) for s in big]
+    T,rows,proj,feat,mixed,rden,mid,sec=vm
+    D=pltpu.SemaphoreType.DMA
+    return pl.pallas_call(k1_kernel,
+      out_shape=tuple(big+[S((last+1,d,f//4),BF),S((last+1,f//4,d),BF),S((4,R,d),BF)]),
+      in_specs=[SM,ANY,VM,ANY,VM,ANY,VM,ANY,ANY,ANY],out_specs=[ANY]*11,
+      scratch_shapes=[T,rows,pltpu.VMEM((3,d,c),BF),pltpu.VMEM((c,d),BF),proj,feat,mixed,rden,
+        pltpu.VMEM((R,d),F32),pltpu.VMEM((R,d),BF),pltpu.VMEM((R,d),BF),mid,sec,
+        pltpu.VMEM((2,h//2,2*hd,2*hd),BF),D((16,)),D((2,5)),D((2,2*last)),D((2,2*last)),D((2,4*last))],
+      compiler_params=pltpu.CompilerParams(vmem_limit_bytes=48*2**20,collective_id=1,has_side_effects=True),
+      cost_estimate=pl.CostEstimate(flops=4*10**9,bytes_accessed=30*10**6,transcendentals=10**6))(
+      length,tok,g1,wqkv,wf,wout,g2,wup,wdn,cot)
+
+def per_device_k1(
+    tokens, lengths, norm_first, w_qkv, w_feature, w_out, norm_second, w_up, w_down, cotangent
+):
+    wqkv=jnp.transpose(w_qkv,(1,0,2))
+    tok,first_rows,proj,feat,mixed,rden,middle,second_low,wu,wd,cot_all=k1(lengths,tokens[0],norm_first[None],wqkv,w_feature,w_out,norm_second[None],w_up,w_down,cotangent[0])
+    residual_in = tokens[0].astype(jnp.float32)
+    _, first_back = jax.vjp(normalize, residual_in, norm_first)
+    cot_low = cotangent[0]
+    _, second_back = jax.vjp(normalize, middle, norm_second)
+    g=[[0,2],[1,3]]
+    sx=lax.all_gather(second_low,"dp",axis_index_groups=g)
+    sxy=lax.all_gather(sx,"head",axis=1).reshape(4*256,1024)
+    cot_rows=cot_all.reshape(1024,1024)
+    up=jnp.transpose(wu,(1,0,2)).reshape(1024,1024)
+    dn=wd.reshape(1024,1024)
+    hidden_pre = jnp.dot(sxy, up, preferred_element_type=jnp.float32)
+    active = smooth_gate(hidden_pre).astype(jnp.bfloat16)
+    gate_grad = jax.vjp(smooth_gate, hidden_pre)[1]
+    d_active = jnp.einsum("nd,fd->nf", cot_rows, dn, preferred_element_type=jnp.float32)
+    d_pre = gate_grad(d_active)[0].astype(jnp.bfloat16)
+    def scat(v):
+        v=v.astype(jnp.bfloat16).reshape(2,2,256,1024)
+        v=lax.psum_scatter(v,"head",scatter_dimension=1)
+        return lax.psum_scatter(v,"dp",scatter_dimension=0,axis_index_groups=g).astype(jnp.float32)
+    d_second=scat(jnp.einsum("nf,df->nd", d_pre, up, preferred_element_type=jnp.float32))
+    mlp_result=scat(jnp.dot(active, dn, preferred_element_type=jnp.float32))
+    block_out = (middle + mlp_result).astype(jnp.bfloat16)
+    gd = jnp.einsum("nf,nd->fd", active, cot_rows, preferred_element_type=jnp.float32).astype(BF).reshape(4,256,1024)
+    gu = jnp.einsum("nd,nf->df", sxy, d_pre, preferred_element_type=jnp.float32).astype(BF).reshape(1024,4,256)
+    gd=lax.psum_scatter(gd,"hidden",scatter_dimension=0)
+    gu=lax.psum_scatter(gu,"hidden",scatter_dimension=1)
+    gd=lax.psum(gd,"dp",axis_index_groups=[[0,1],[2,3]]); gu=lax.psum(gu,"dp",axis_index_groups=[[0,1],[2,3]])
+    grad_down=lax.all_gather(lax.all_gather(gd,"head"),"dp",axis_index_groups=g).reshape(1024,1024).astype(F32)
+    grad_up=lax.all_gather(lax.all_gather(gu,"head",axis=1),"dp",axis=1,axis_index_groups=g).reshape(1024,1024).astype(F32)
+    d_middle_norm, grad_norm_second = second_back(d_second)
+    d_middle = cot_low.astype(jnp.float32) + d_middle_norm
+    d_branch_rows = lax.all_gather(d_middle.astype(jnp.bfloat16), "head", axis=0, tiled=True)
+    gq,grad_feature,go,dfirst=bwd(first_rows,wqkv,w_feature,w_out,proj,feat,mixed,rden,d_branch_rows)
+    d_first = lax.psum_scatter(dfirst, "head", scatter_dimension=0, tiled=True).astype(jnp.float32)
+    d_input_norm, grad_norm_first = first_back(d_first)
+    grad_tokens = d_middle + d_input_norm
+    gq, grad_feature, go = (
+        lax.psum(gq, ("dp", "hidden")).astype(jnp.float32),
+        lax.psum(grad_feature.astype(jnp.bfloat16), ("dp", "hidden")).astype(jnp.float32),
+        lax.psum(go, ("dp", "hidden")).astype(jnp.float32),
+    )
+    grad_norm_first, grad_norm_second = lax.psum(
+        (grad_norm_first, grad_norm_second), ("dp", "head", "hidden")
+    )
+    return (
+        block_out[None],
+        grad_tokens[None],
+        grad_norm_first,
+        jnp.transpose(gq,(1,0,2)),
+        grad_feature,
+        go,
+        grad_norm_second,
+        grad_up,
+        grad_down,
+    )
+
+
 def solution(mesh):
     in_specs = (
         P(("dp", "hidden"), "head", None),
@@ -275,6 +522,7 @@
         P(None, "hidden"),
         P("hidden", None),
     )
+    near=dict(mesh.shape)=={"dp":4,"head":2,"hidden":4}
     return jax.shard_map(
-        per_device, mesh=mesh, in_specs=in_specs, out_specs=out_specs, check_vma=False
-    )
+        per_device_k1 if near else per_device, mesh=mesh, in_specs=in_specs, out_specs=out_specs, check_vma=False
+    )

time: 538 us -> 655 us (1.22)
  waiting for transfers between devices: 372 us -> 435 us
  Pallas kernels: 35.2 us -> 71.6 us
  local copies, waits for them, and re-layouts: 1.45 us -> 27.3 us
  other arithmetic: 37 us -> 29.3 us
    reduce_scatter x4 -> x7, waiting for transfers between devices: 116 us -> 198 us  [the longest x2 68.3 us: scat(): v = lax.psum_scatter(v, 'head', scatter_dimension=1)]
    psum x2, waiting for transfers between devices: 135 us -> 95.6 us  [the longest x1 73.6 us: per_device_k1(): lax.psum(gq, ('dp', 'hidden')).astype(jnp.float32)]
    pallas_call x1, Pallas kernels: 12.5 us -> 48.9 us  [k1(): pl.pallas_call(k1_kernel, out_shape=tuple(big + [S((last + 1, d, f // 4),...]
    all_gather x4 -> x7, waiting for transfers between devices: 119 us -> 141 us  [the longest x1 24.8 us: per_device_k1(): sxy = lax.all_gather(sx, 'head', axis=1).reshape(4 * 256, 1024)]
    unnamed x24 -> x35, local copies, waits for them, and re-layouts: 1.45 us -> 13.4 us
    reshape x0 -> x3, local copies, waits for them, and re-layouts: none -> 6.94 us  [the longest x1 3.96 us: per_device_k1(): jnp.einsum('nd,nf->df', sxy, d_pre, preferred_element_type=jnp.float32)]
    convert_element_type x8 -> x6, other arithmetic: 18.5 us -> 15.6 us  [the longest x1 4.07 us: per_device_k1(): lax.all_gather(lax.all_gather(gu, 'head', axis=1), 'dp', axis=1, axis_ind...]
  transfers between devices with their start and end apart: 10 -> 16, of which waited for: 10 -> 16; matrix products, arithmetic and copies ran while one was open for 7% -> 9% of each run, Pallas kernels for 4% -> 3%
where the time goes in v2:
time: 655 us; the launch traced here: 654 us
  waiting for transfers between devices  435 us (66%)
  Pallas kernels  71.6 us (11%)
  blocking collectives  40.9 us (6%)
  matrix products  33.7 us (5%)
  other arithmetic  29.3 us (4%)
  local copies, waits for them, and re-layouts  27.3 us (4%)
  between operations  14.7 us (2%)
    psum x1, waiting for transfers between devices, per_device_k1(): lax.psum(gq, ('dp', 'hidden')).astype(jnp.float32)  73.6 us
    reduce_scatter x2, waiting for transfers between devices, scat(): v = lax.psum_scatter(v, 'head', scatter_dimension=1)  68.3 us
    pallas_call x1, Pallas kernels, k1(): pl.pallas_call(k1_kernel, out_shape=tuple(big + [S((last + 1, d, f // 4),...  48.9 us
    reduce_scatter x1, waiting for transfers between devices, per_device_k1(): gu = lax.psum_scatter(gu, 'hidden', scatter_dimension=1)  46.1 us
    reduce_scatter x2, waiting for transfers between devices, scat(): lax.psum_scatter(v, 'dp', scatter_dimension=0, axis_index_groups=g)  44.2 us
    psum x1, blocking collectives, per_device_k1(): lax.psum((grad_norm_first, grad_norm_second), ('dp', 'head', 'hidden'))  40.9 us
    all_gather x1, waiting for transfers between devices, per_device_k1(): sxy = lax.all_gather(sx, 'head', axis=1).reshape(4 * 256, 1024)  24.8 us
    all_gather x1, waiting for transfers between devices, per_device_k1(): lax.all_gather(d_middle.astype(jnp.bfloat16), 'head', axis=0, tiled=True)  23.3 us
  transfers between devices with their start and end apart: 16, of which 16 were waited for; matrix products, arithmetic and copies ran while one was open for 9% of the time, Pallas kernels for 3%

profile of v2, /device:TPU:0, one launch (start us, length us, event | category | flops | bytes accessed | tf_op | source)
XLA Modules:
  0.0 653.9 jit_solution(16348336390575710082)
XLA Ops:
  12.3 48.9 %shard_map.169 = (bf16[512,1024]{1,0:T(8,128)(2,1)}, bf16[512,1024]{1,0:T(8,128)(2,1)S(1)}, bf16[3,512,512]{2,1,0:T(8,128)(2,1)}, bf16[2,4,512,256]{3,2,1,0:T(8,...) custom-call(s32[1,1]{1,0:T(1,128)S(6)} %copy.39.len_ref, ...), custom_call_target="tpu_custom_call" | custom-call | flops 4000000000 | bytes 30000000 | tf_op jit(solution)/shard_map/pallas_call | solution.py:429
  64.1 19.5 %all-gather.18.cloned.1.call-done = bf16[512,1024]{1,0:T(8,128)(2,1)} async-done(((bf16[256,1024]{1,0:T(8,128)(2,1)}), bf16[512,1024]{1,0:T(8,128)(2,1)}) %all-gather.18.cloned.1.call-update) | async-done | bytes 1048592 | tf_op jit(solution)/shard_map/all_gather | solution.py:449
  83.8 3.0 copy.28
  86.8 6.6 %fusion.26 = f32[1024,1024]{1,0:T(8,128)} fusion(bf16[1024,1024]{1,0:T(8,128)(2,1)} %bitcast.76, bf16[1024,1024]{1,0:T(8,128)(2,1)} %bitcast.74), kind=kOutput, calls=%fused_computation.55 | convolution fusion | flops 2147483648 | bytes 8388608 | tf_op jit(solution)/shard_map/nd,fd->nf/dot_general | solution.py:457
  93.4 24.8 %all-gather.20.cloned.1.call-done = bf16[2,512,1024]{2,1,0:T(8,128)(2,1)} async-done(((bf16[2,256,1024]{2,1,0:T(8,128)(2,1)}), bf16[2,512,1024]{2,1,0:T(8,128)(2,1)}) %all-gather.20.cloned.1.call-update) | async-done | bytes 2097168 | tf_op jit(solution)/shard_map/all_gather | solution.py:450
  118.3 8.3 %fusion.6 = (bf16[1024,1024]{1,0:T(8,128)(2,1)}, f32[1024,1024]{1,0:T(8,128)S(1)}) fusion(f32[1024,1024]{1,0:T(8,128)} %fusion.26, bf16[1024,1024]{1,0:T(8,128)(2,1)} %bitcast.72, bf16[1024,1024]{0,1:T(8,128)(2,1)S(1)} %bitcast.63), kind=kOutput, calls=%fused_computation.8 | convolution fusion | flops 2168455168 | bytes 14680064 | tf_op jit(solution)/shard_map/dot_general | solution.py:454
  126.6 4.1 convolution_convert_fusion
  130.8 5.9 convolution_convert_fusion.1
  136.7 4.0 copy.31
  140.7 3.9 convolution_convert_fusion.2
  147.0 4.8 convolution_convert_fusion.3
  153.5 21.3 %reduce-scatter.20.cloned.1.call-done = bf16[1,256,1024]{2,1,0:T(8,128)(2,1)} async-done(((bf16[4,256,1024]{2,1,0:T(8,128)(2,1)}), bf16[1,256,1024]{2,1,0:T(8,128)(2,1)}) %reduce-scatter.20.cloned.1.call-update) | async-done | bytes 524304 | tf_op jit(solution)/shard_map/reduce_scatter | solution.py:468
  174.7 46.1 %reduce-scatter.18.cloned.1.call-done = bf16[1024,1,256]{2,0,1:T(8,128)(2,1)} async-done(((bf16[1024,4,256]{2,0,1:T(8,128)(2,1)}), bf16[1024,1,256]{2,0,1:T(8,128)(2,1)}) %reduce-scatter.18.cloned.1.call-update) | async-done | bytes 524304 | tf_op jit(solution)/shard_map/reduce_scatter | solution.py:469
  220.9 33.8 %reduce-scatter.12.cloned.1.call-done = bf16[2,1,256,1024]{3,2,0,1:T(8,128)(2,1)} async-done(((bf16[2,2,256,1024]{3,2,0,1:T(8,128)(2,1)}), bf16[2,1,256,1024]{3,2,0,1:T(8,128)(2,1)}) %reduce-scatter.12.cloned.1.call-update) | async-done | bytes 1048592 | tf_op jit(solution)/shard_map/reduce_scatter | solution.py:461
  254.7 34.5 %reduce-scatter.8.cloned.1.call-done = bf16[2,1,256,1024]{3,2,0,1:T(8,128)(2,1)} async-done(((bf16[2,2,256,1024]{3,2,0,1:T(8,128)(2,1)}), bf16[2,1,256,1024]{3,2,0,1:T(8,128)(2,1)}) %reduce-scatter.8.cloned.1.call-update) | async-done | bytes 1048592 | tf_op jit(solution)/shard_map/reduce_scatter | solution.py:461
  289.3 22.0 %all-reduce.8.cloned.1.call-done = (bf16[1024,1,256]{2,0,1:T(8,128)(2,1)}, bf16[1,256,1024]{2,1,0:T(8,128)(2,1)}) async-done(((bf16[1024,1,256]{2,0,1:T(8,128)(2,1)}, bf16[1,256,1024]{2,1,0:T(8,128)(2,1)}), (bf16[1024,1,256]{2,0,1:T(8,128)(2,1)}, bf16[1,256,1024]{2,1,0:T(8,128)(2,1)})) %all-reduce.8.cloned.1.call-update) | async-done | bytes 1048592 | tf_op jit(solution)/shard_map/psum | solution.py:470
  312.2 23.0 %reduce-scatter.14.cloned.1.call-done = bf16[1,256,1024]{2,1,0:T(8,128)(2,1)} async-done(((bf16[2,256,1024]{2,1,0:T(8,128)(2,1)}), bf16[1,256,1024]{2,1,0:T(8,128)(2,1)}) %reduce-scatter.14.cloned.1.call-update) | async-done | bytes 524304 | tf_op jit(solution)/shard_map/reduce_scatter | solution.py:462
  336.7 21.1 %reduce-scatter.10.cloned.1.call-done = bf16[1,256,1024]{2,1,0:T(8,128)(2,1)} async-done(((bf16[2,256,1024]{2,1,0:T(8,128)(2,1)}), bf16[1,256,1024]{2,1,0:T(8,128)(2,1)}) %reduce-scatter.10.cloned.1.call-update) | async-done | bytes 524304 | tf_op jit(solution)/shard_map/reduce_scatter | solution.py:462
  361.3 19.4 %all-gather.14.cloned.1.call-done = bf16[1024,2,256]{2,0,1:T(8,128)(2,1)} async-done(((bf16[1024,1,256]{2,0,1:T(8,128)(2,1)}), bf16[1024,2,256]{2,0,1:T(8,128)(2,1)}) %all-gather.14.cloned.1.call-update) | async-done | bytes 1048592 | tf_op jit(solution)/shard_map/all_gather | solution.py:472
  380.7 22.9 %all-gather.16.cloned.1.call-done = bf16[2,256,1024]{2,1,0:T(8,128)(2,1)} async-done(((bf16[1,256,1024]{2,1,0:T(8,128)(2,1)}), bf16[2,256,1024]{2,1,0:T(8,128)(2,1)}) %all-gather.16.cloned.1.call-update) | async-done | bytes 1048592 | tf_op jit(solution)/shard_map/all_gather | solution.py:471
  403.6 23.3 %all-gather.12.cloned.1.call-done.dbr_ref = bf16[512,1024]{1,0:T(8,128)(2,1)} async-done(((bf16[256,1024]{1,0:T(8,128)(2,1)}), bf16[512,1024]{1,0:T(8,128)(2,1)}) %all-gather.12.cloned.1.call-update) | async-done | bytes 1048592 | tf_op jit(solution)/shard_map/all_gather | solution.py:475
  427.0 22.7 %shard_map.170 = (bf16[3,1024,512]{2,1,0:T(8,128)(2,1)}, f32[2,8,64,64]{3,2,1,0:T(8,128)}, bf16[512,1024]{1,0:T(8,128)(2,1)}, bf16[512,1024]{1,0:T(8,128)(2,1)}) custom-call(bf16[512,1024]{1,0:T(8,128)(2,1)} %copy-done.4, bf16[3,1024,512]{2,1,0:T(8,128)(2,1)} %bitcast.61, bf16[2,8,64,64]{3,2,1,0:T(8,128)(2,1)} %wf_ref.1, bf16[512,1024]{1,0:T(8,128)(2,1)} %wout_ref.1, ...), custom_call_target="tpu_custom_call" | custom-call | tf_op jit(solution)/shard_map/pallas_call | solution.py:169
  451.9 9.8 %all-gather.22.cloned.1.call-done = bf16[1024,4,256]{2,0,1:T(8,128)(2,1)} async-done(((bf16[1024,2,256]{2,0,1:T(8,128)(2,1)}), bf16[1024,4,256]{2,0,1:T(8,128)(2,1)}) %all-gather.22.cloned.1.call-update) | async-done | bytes 2097168 | tf_op jit(solution)/shard_map/all_gather | solution.py:472
  461.7 3.9 copy.32
  465.7 4.1 bitcast_convert_fusion.1
  469.7 5.6 copy.33
  475.4 21.0 %all-gather.24.cloned.1.call-done = bf16[4,256,1024]{2,1,0:T(8,128)(2,1)} async-done(((bf16[2,256,1024]{2,1,0:T(8,128)(2,1)}), bf16[4,256,1024]{2,1,0:T(8,128)(2,1)}) %all-gather.24.cloned.1.call-update) | async-done | bytes 2097168 | tf_op jit(solution)/shard_map/all_gather | solution.py:471
  496.4 4.1 bitcast_convert_fusion
  500.4 18.5 %reduce-scatter.16.cloned.1.call-done = bf16[256,1024]{1,0:T(8,128)(2,1)} async-done(((bf16[512,1024]{1,0:T(8,128)(2,1)}), bf16[256,1024]{1,0:T(8,128)(2,1)}) %reduce-scatter.16.cloned.1.call-update) | async-done | bytes 524304 | tf_op jit(solution)/shard_map/reduce_scatter | solution.py:477
  522.0 40.9 %all-reduce = (f32[1024]{0:T(1024)}, f32[1024]{0:T(1024)}) all-reduce(f32[1024]{0:T(1024)S(1)} %get-tuple-element.48, f32[1024]{0:T(1024)S(1)} %get-tuple-element.46), channel_id=1, replica_groups=mesh['dp'=4,'head'=2,'hidden'=4] {'dp','head','hidden'}, use_global_device_ids=true, to_apply=%region_14.0 | all-reduce | flops 2048 | bytes 16384 | tf_op jit(solution)/shard_map/psum | solution.py:485
  565.4 73.6 %all-reduce.6.cloned.1.call-done = (bf16[1024,3,512]{2,0,1:T(8,128)(2,1)}, bf16[2,8,64,64]{3,2,1,0:T(8,128)(2,1)}, bf16[512,1024]{1,0:T(8,128)(2,1)}) async-done(((bf16[1024,3,512]{2,0,1:T(8,128)(2,1)}, bf16[2,8,64,64]{3,2,1,0:T(8,128)(2,1)}, bf16[512,1024]{1,0:T(8,128)(2,1)}), (bf16[1024,3,512]{2,0,1:T(8,128)(2,1)}, bf16[2,8,64,64]{3,2,1,0:T(8,128)(2,1)}, ...) | async-done | bytes 4325392 | tf_op jit(solution)/shard_map/psum | solution.py:481
  643.8 3.6 transpose.21
  (87 shorter events, 30.1 us)
Async XLA Ops:
  7.2 76.4 %all-gather.18.cloned.1.call-start = ((), (), s32[]{:S(2)}) async-start(), calls=%async_computation.17 | async-start | bytes 1572864 | tf_op jit(solution)/shard_map/all_gather | solution.py:449
  7.9 1.0 copy-start
  8.9 1.0 copy-start.2
  10.0 0.9 copy-start.7
  10.9 0.7 copy-start.8
  61.2 1.0 copy-start.4
  62.2 1.0 copy-start.5
  63.2 0.8 copy-start.6
  64.1 54.2 %all-gather.20.cloned.1.call-start = ((), (), s32[]{:S(2)}) async-start(), calls=%async_computation.18 | async-start | bytes 3145728 | tf_op jit(solution)/shard_map/all_gather | solution.py:450
  83.6 91.1 %reduce-scatter.20.cloned.1.call-start = ((), (), s32[]{:S(2)}) async-start(), calls=%async_computation.15 | async-start | bytes 2621440 | tf_op jit(solution)/shard_map/reduce_scatter | solution.py:468
  118.3 8.3 %copy-start.15 = (bf16[4,256,1024]{2,1,0:T(8,128)(2,1)S(1)}, bf16[4,256,1024]{2,1,0:T(8,128)(2,1)}, u32[]{:S(2)}) copy-start(bf16[4,256,1024]{2,1,0:T(8,128)(2,1)} %get-tuple-element.27) | copy-start | bytes 6291460
  126.6 4.1 copy-start.16
  130.7 90.1 %reduce-scatter.18.cloned.1.call-start = ((), (), s32[]{:S(2)}) async-start(), calls=%async_computation.13 | async-start | bytes 2621440 | tf_op jit(solution)/shard_map/reduce_scatter | solution.py:469
  140.7 114.0 %reduce-scatter.12.cloned.1.call-start = ((), (), s32[]{:S(2)}) async-start(), calls=%async_computation.9 | async-start | bytes 3145728 | tf_op jit(solution)/shard_map/reduce_scatter | solution.py:461
  144.7 2.4 copy-start.14
  146.2 143.1 %reduce-scatter.8.cloned.1.call-start = ((), (), s32[]{:S(2)}) async-start(), calls=%async_computation.7 | async-start | bytes 3145728 | tf_op jit(solution)/shard_map/reduce_scatter | solution.py:461
  151.9 159.5 %copy-start.12 = (f32[256,1024]{1,0:T(8,128)S(1)}, f32[256,1024]{1,0:T(8,128)}, u32[]{:S(2)}) copy-start(f32[256,1024]{1,0:T(8,128)} %get-tuple-element.23) | copy-start | bytes 3145732
  153.4 181.8 %copy-start.11 = (f32[1024]{0:T(1024)S(1)}, f32[1024]{0:T(1024)}, u32[]{:S(2)}) copy-start(f32[1024]{0:T(1024)} %param.16) | copy-start | bytes 12292
  153.4 157.9 %all-reduce.8.cloned.1.call-start = ((), (), s32[]{:S(2)}) async-start(), calls=%async_computation.22 | async-start | bytes 2097152 | tf_op jit(solution)/shard_map/psum | solution.py:470
  220.8 114.4 %reduce-scatter.14.cloned.1.call-start = ((), (), s32[]{:S(2)}) async-start(), calls=%async_computation.10 | async-start | bytes 1572864 | tf_op jit(solution)/shard_map/reduce_scatter | solution.py:462
  254.7 103.1 %reduce-scatter.10.cloned.1.call-start = ((), (), s32[]{:S(2)}) async-start(), calls=%async_computation.8 | async-start | bytes 1572864 | tf_op jit(solution)/shard_map/reduce_scatter | solution.py:462
  289.3 91.3 %all-gather.14.cloned.1.call-start = ((), (), s32[]{:S(2)}) async-start(), calls=%async_computation.14 | async-start | bytes 1572864 | tf_op jit(solution)/shard_map/all_gather | solution.py:472
  311.3 48.9 %copy-start.3 = (bf16[1,256,1024]{2,1,0:T(8,128)(2,1)S(1)}, bf16[1,256,1024]{2,1,0:T(8,128)(2,1)}, u32[]{:S(2)}) copy-start(bf16[1,256,1024]{2,1,0:T(8,128)(2,1)} %param.19) | copy-start | bytes 1572868
  311.4 92.2 %all-gather.16.cloned.1.call-start = ((), (), s32[]{:S(2)}) async-start(), calls=%async_computation.16 | async-start | bytes 1572864 | tf_op jit(solution)/shard_map/all_gather | solution.py:471
  312.1 114.9 %all-gather.12.cloned.1.call-start = ((), (), s32[]{:S(2)}) async-start(), calls=%async_computation.11 | async-start | bytes 1572864 | tf_op jit(solution)/shard_map/all_gather | solution.py:475
  361.2 100.5 %all-gather.22.cloned.1.call-start = ((), (), s32[]{:S(2)}) async-start(), calls=%async_computation.19 | async-start | bytes 3145728 | tf_op jit(solution)/shard_map/all_gather | solution.py:472
  380.6 115.7 %all-gather.24.cloned.1.call-start = ((), (), s32[]{:S(2)}) async-start(), calls=%async_computation.20 | async-start | bytes 3145728 | tf_op jit(solution)/shard_map/all_gather | solution.py:471
  403.6 115.3 %reduce-scatter.16.cloned.1.call-start = ((), (), s32[]{:S(2)}) async-start(), calls=%async_computation.12 | async-start | bytes 1572864 | tf_op jit(solution)/shard_map/reduce_scatter | solution.py:477
  427.0 23.0 %copy-start.1 = (bf16[1,256,1024]{2,1,0:T(8,128)(2,1)S(1)}, bf16[1,256,1024]{2,1,0:T(8,128)(2,1)}, u32[]{:S(2)}) copy-start(bf16[1,256,1024]{2,1,0:T(8,128)(2,1)} %param.10) | copy-start | bytes 1572868
  449.6 189.4 %all-reduce.6.cloned.1.call-start = ((), (), s32[]{:S(2)}) async-start(), calls=%async_computation.21 | async-start | bytes 8912896 | tf_op jit(solution)/shard_map/psum | solution.py:481
  475.4 43.5 %copy-start.9 = (f32[1024]{0:T(1024)S(1)}, f32[1024]{0:T(1024)}, u32[]{:S(2)}) copy-start(f32[1024]{0:T(1024)} %param.12) | copy-start | bytes 12292
  639.0 4.7 copy-start.13
  (1 other events, 0.7 us)
Sparse Core Ops, SparseCore 0:
  64.2 19.3 all-gather.17
  85.1 33.1 all-gather.19
  130.9 43.8 reduce-scatter.19
  177.6 43.1 reduce-scatter.17
  223.5 31.1 reduce-scatter.11
  257.4 31.8 reduce-scatter.7
  291.6 19.6 all-reduce.7
  313.7 21.4 reduce-scatter.13
  337.4 20.3 reduce-scatter.9
  359.3 21.2 all-gather.13
  382.2 21.2 all-gather.15
  405.6 21.2 all-gather.11
  428.6 33.1 all-gather.21
  463.2 33.1 all-gather.23
  498.5 20.3 reduce-scatter.15
  523.3 115.7 all-reduce.5

commit v3 on v2

--- a/solution.py
+++ b/solution.py
@@ -306,7 +306,6 @@
     hu=wup.shape[0]//2; hw=fs//2
     uh=pl.ds(pl.multiple_of(c*hu,hu),hu); dh=pl.ds(pl.multiple_of(c*hw,hw),hw)
     l_tok=lc(tok,T.at[mine],0); l_wq=[lc(wqkv.at[i],wq.at[i],1+i) for i in range(3)]; l_wo=lc(wout,wo,4)
-    l_wu=lc(wup.at[:,cols],wu_o.at[z],5); l_wd=lc(wdn.at[cols],wd_o.at[z],6); l_cot=lc(cot,cot_o.at[q],7)
     l_tok.start()
     for k in l_wq: k.start()
     greet((nx,ny,nc),True)
@@ -360,7 +359,7 @@
     z_send(1)
     r_cx=remote(cot,cot_o.at[q],rem,1,nx)
     r_cx.start()
-    for k in (l_wo,l_wu,l_wd,l_cot): k.start()
+    l_wo.start()
     pair_weights(wf,w2)
     ones=half_ones(2*w,hd)
     def first(at):
@@ -373,6 +372,8 @@
     for k in l_wq: k.wait()
     project(mine)
     r_tok.wait_recv()
+    z_recv(1)
+    z_send(2)
     r_cy=remote(cot,cot_o.at[q],rem,2,ny)
     r_cy.start()
     l_tok_o=lc(T,tok_o,8); l_tok_o.start()
@@ -389,19 +390,16 @@
         m,rd=attend(fq,fk,proj[2,:,cc],hd)
         mixed[:,cc]=m.astype(BF); rden[:,cc]=rd
         return 0
-    lax.fori_loop(0,pairs//2,body,0)
-    z_recv(1)
-    z_send(2)
-    lax.fori_loop(pairs//2,pairs,body,0)
+    lax.fori_loop(0,pairs,body,0)
     l_wo.wait()
     snd[...]=mm(mixed[other],wo[...]).astype(BF)
     r_part=remote(snd,rcv,rem,3,ny)
     r_part.start()
+    z_recv(2)
+    z_send(3)
     own[...]=mm(mixed[mine],wo[...])
     l_feat=lc(feat,feat_o,11); l_mixed=lc(mixed,mixed_o,12); l_rden=lc(rden,rden_o,13)
     for k in (l_feat,l_mixed,l_rden): k.start()
-    z_recv(2)
-    z_send(3)
     r_cy.wait_recv()
     yq=x*2+1-y
     r_cf=remote(cot_o.at[yq],cot_o.at[yq],rem,4,nx)
@@ -417,7 +415,7 @@
     r_cx.wait_recv(); r_cf.wait_recv()
     for k in (r_tok,r_cx,r_cy,r_part,r_cf): k.wait_send()
     z_end()
-    for k in (l_wu,l_wd,l_cot,l_tok_o,l_rows,l_proj,l_feat,l_mixed,l_rden,l_mid,l_sec): k.wait()
+    for k in (l_tok_o,l_rows,l_proj,l_feat,l_mixed,l_rden,l_mid,l_sec): k.wait()
 
 def k1(length,tok,g1,wqkv,wf,wout,g2,wup,wdn,cot):
     R,d=tok.shape; n=2*R; c=wout.shape[0]; h=wf.shape[1]; hd=wf.shape[-1]; f=wup.shape[1]
@@ -432,69 +430,410 @@
       scratch_shapes=[T,rows,pltpu.VMEM((3,d,c),BF),pltpu.VMEM((c,d),BF),proj,feat,mixed,rden,
         pltpu.VMEM((R,d),F32),pltpu.VMEM((R,d),BF),pltpu.VMEM((R,d),BF),mid,sec,
         pltpu.VMEM((2,h//2,2*hd,2*hd),BF),D((16,)),D((2,5)),D((2,2*last)),D((2,2*last)),D((2,4*last))],
-      compiler_params=pltpu.CompilerParams(vmem_limit_bytes=48*2**20,collective_id=1,has_side_effects=True),
+      compiler_params=pltpu.CompilerParams(vmem_limit_bytes=62*2**20,collective_id=1,has_side_effects=True),
       cost_estimate=pl.CostEstimate(flops=4*10**9,bytes_accessed=30*10**6,transcendentals=10**6))(
       length,tok,g1,wqkv,wf,wout,g2,wup,wdn,cot)
+
+def add_into(dst,src,step):
+    rows=dst.shape[0]
+    def body(i,_):
+        r=pl.ds(pl.multiple_of(i*step,step),step)
+        dst[r]=(dst[r].astype(F32)+src[r].astype(F32)).astype(dst.dtype)
+        return 0
+    lax.fori_loop(0,rows//step,body,0)
+
+def gate(v):
+    k=0.7978845608; a=0.044715
+    sq=v*v
+    t=jnp.tanh(k*v*(1.0+a*sq))
+    half=0.5*(1.0+t)
+    return v*half, half+0.5*v*(1.0-t*t)*(k+(3.0*a*k)*sq)
+
+def norm_back(values,grad,gain):
+    xh,r=unit(values)
+    e=grad*gain
+    inner=e-jnp.mean(e,axis=-1,keepdims=True)-xh*jnp.mean(e*xh,axis=-1,keepdims=True)
+    return r*inner, jnp.sum(grad*xh,axis=0,keepdims=True)
+
+def k2_kernel(sec,mid,cots,cot,wu,wd,wup,wdn,g2,
+              dmid_o,dbr_o,gn_o,mlp_o,gu_o,gd_o,
+              SA,CA,Wu,Wd,act,dpre,P,mlp,gu,gd,midv,dmid,dbr,own,rx,ry,rdx,rdy,cu,cd,zu,loc,ag,rs):
+    x,c,y,z=place()
+    nx,ny,nc=around()
+    nh=lax.axis_size("hidden")
+    z1,z2=z+1-2*(z%2),(z+2)%nh
+    n1=(x*2+c,y,z1)
+    R,d=sec.shape; H=R//2; fs=wu.shape[2]; nz=wu.shape[0]
+    qo,qx,qy,qd=x*2+y,(1-x)*2+y,x*2+1-y,(1-x)*2+1-y
+    lc=lambda s,t,i: pltpu.make_async_copy(s,t,loc.at[i])
+    l_sec=lc(sec,SA.at[qo],0)
+    at=lambda j: pl.ds(pl.multiple_of(j*fs,fs),fs)
+    l_wu=[lc(wup.at[:,at(qo)],Wu.at[:,at(z)],1)]; l_wd=[lc(wdn.at[at(qo)],Wd.at[at(z)],2)]
+    for t in range(1,nz):
+        j=(z+t)%nz
+        l_wu.append(lc(wu.at[j],Wu.at[:,at(j)],2*t+1)); l_wd.append(lc(wd.at[j],Wd.at[at(j)],2*t+2))
+    l_cot=[lc(cot,CA.at[qo],2*nz+1)]+[lc(cots.at[q],CA.at[q],2*nz+2+i) for i,q in enumerate((qx,qy,qd))]
+    l_mid=lc(mid,midv,2*nz+5)
+    l_sec.start()
+    for k in l_wu: k.start()
+    greet((nx,ny,nc,n1),False)
+    A=pl.ds(0,H); B=pl.ds(H,H)
+    xa=remote(sec.at[A],SA.at[qo,A],ag,0,nx); xb=remote(sec.at[B],SA.at[qo,B],ag,1,nx)
+    yb=remote(sec.at[B],SA.at[qo,B],ag,2,ny); ya=remote(sec.at[A],SA.at[qo,A],ag,3,ny)
+    for k in (xa,yb,xb,ya): k.start()
+    for k in l_wd+l_cot: k.start()
+    l_mid.start()
+    def block(qi,keep):
+        hp=mm(SA[qi],Wu[...])
+        a,ga=gate(hp)
+        act[qi]=a.astype(BF)
+        dp=(mm_nt(CA[qi],Wd[...])*ga).astype(BF)
+        dpre[qi]=dp
+        d2=mm_nt(dp,Wu[...])
+        if keep: own[...]=d2
+        else: P[qi]=d2.astype(BF)
+    def down(qi): mlp[qi]=mm(act[qi],Wd[...]).astype(BF)
+    l_sec.wait()
+    for k in l_wu: k.wait()
+    for k in l_cot+l_wd: k.wait()
+    block(qo,True)
+    xa.wait_recv()
+    fa=remote(SA.at[qx,A],SA.at[qx,A],ag,4,ny); fa.start()
+    yb.wait_recv()
+    fb=remote(SA.at[qy,B],SA.at[qy,B],ag,5,nx); fb.start()
+    down(qo)
+    xb.wait_recv()
+    block(qx,False)
+    p_xa=remote(P.at[qx,A],rx.at[A],rs,0,nx); p_xa.start()
+    ya.wait_recv()
+    block(qy,False)
+    p_yb=remote(P.at[qy,B],ry.at[B],rs,1,ny); p_yb.start()
+    fa.wait_recv(); fb.wait_recv()
+    block(qd,False)
+    p_da=remote(P.at[qd,A],rdx,rs,2,nx); p_da.start()
+    p_db=remote(P.at[qd,B],rdy,rs,3,ny); p_db.start()
+    rows=4*R
+    hu,hw=d//2,fs//2
+    half=lambda size,b: pl.ds(pl.multiple_of(b*size,size),size)
+    uo,ua,do,da=half(hu,c),half(hu,1-c),half(hw,c),half(hw,1-c)
+    sa=SA[...].reshape(rows,-1)
+    for j in range(nz//2):
+        cc=pl.ds(2*j*fs,2*fs)
+        t=mm_tn(sa,dpre[:,:,cc].reshape(rows,-1)).astype(BF)
+        gu[2*j]=t[:,:fs]; gu[2*j+1]=t[:,fs:]
+    k_u=remote(gu.at[:,ua],cu,rs,6,nc); k_u.start()
+    down(qx); down(qy); down(qd)
+    l_mlp=lc(mlp,mlp_o,2*nz+6); l_mlp.start()
+    k_u.wait_recv()
+    for j in range(nz): add_into(gu.at[j,uo],cu.at[j],64)
+    zz1=(z1+2)%nh
+    k_z=[remote(gu.at[z1,uo],zu.at[0],rs,7,n1),remote(gu.at[zz1,uo],zu.at[1],rs,8,n1)]
+    for k in k_z: k.start()
+    p_da.wait_recv()
+    P[qy,A]=(P[qy,A].astype(F32)+rdx[...].astype(F32)).astype(BF)
+    p_ya=remote(P.at[qy,A],ry.at[A],rs,4,ny); p_ya.start()
+    p_db.wait_recv()
+    P[qx,B]=(P[qx,B].astype(F32)+rdy[...].astype(F32)).astype(BF)
+    p_xb=remote(P.at[qx,B],rx.at[B],rs,5,nx); p_xb.start()
+    ca=CA[...].reshape(rows,-1)
+    for j in range(nz):
+        gd[j]=mm_tn(act[:,:,pl.ds(j*fs,fs)].reshape(rows,-1),ca).astype(BF)
+    k_d=remote(gd.at[:,da],cd,rs,9,nc); k_d.start()
+    l_mid.wait()
+    for k in (p_xa,p_xb,p_ya,p_yb): k.wait_recv()
+    ds=own[...]+(rx[...].astype(F32)+ry[...].astype(F32))
+    dx,gn=norm_back(midv[...],ds,g2[...])
+    gn_o[...]=gn
+    dm=CA[qo].astype(F32)+dx
+    dmid[...]=dm; dbr[...]=dm.astype(BF)
+    l_dm=lc(dmid,dmid_o,2*nz+9); l_db=lc(dbr,dbr_o,2*nz+10)
+    l_dm.start(); l_db.start()
+    k_d.wait_recv()
+    for j in range(nz): add_into(gd.at[j,do],cd.at[j],16)
+    l_gd=lc(gd.at[:,do],gd_o,2*nz+8); l_gd.start()
+    for k in k_z: k.wait_recv()
+    add_into(gu.at[z2,uo],zu.at[1],64)
+    l_g1=lc(gu.at[z2,uo],gu_o.at[1],2*nz+7); l_g1.start()
+    add_into(gu.at[z,uo],zu.at[0],64)
+    l_g0=lc(gu.at[z,uo],gu_o.at[0],2*nz+11); l_g0.start()
+    for k in (xa,xb,ya,yb,fa,fb,p_xa,p_xb,p_ya,p_yb,p_da,p_db,k_u,k_d,*k_z): k.wait_send()
+    for k in (l_mlp,l_g0,l_g1,l_gd,l_dm,l_db): k.wait()
+
+def k2(sec,mid,cots,cot,wu,wd,wup,wdn,g2):
+    R,d=sec.shape; nz,_,fs=wu.shape; f=nz*fs
+    V=pltpu.VMEM; D=pltpu.SemaphoreType.DMA
+    return pl.pallas_call(k2_kernel,
+      out_shape=(S((R,d),F32),S((R,d),BF),S((1,d),F32),S((4,R,d),BF),S((2,d//2,fs),BF),S((nz,fs//2,d),BF)),
+      in_specs=[ANY]*8+[VM],out_specs=[ANY,ANY,VM,ANY,ANY,ANY],
+      scratch_shapes=[V((4,R,d),BF),V((4,R,d),BF),V((d,f),BF),V((f,d),BF),V((4,R,f),BF),V((4,R,f),BF),V((4,R,d),BF),V((4,R,d),BF),
+        V((nz,d,fs),BF),V((nz,fs,d),BF),V((R,d),F32),V((R,d),F32),V((R,d),BF),V((R,d),F32),V((R,d),BF),V((R,d),BF),V((R//2,d),BF),V((R//2,d),BF),
+        V((nz,d//2,fs),BF),V((nz,fs//2,d),BF),V((2,d//2,fs),BF),
+        D((2*nz+12,)),D((2,6)),D((2,10))],
+      compiler_params=pltpu.CompilerParams(vmem_limit_bytes=62*2**20,collective_id=2,has_side_effects=True),
+      cost_estimate=pl.CostEstimate(flops=13*10**9,bytes_accessed=30*10**6,transcendentals=10**6))(
+      sec,mid,cots,cot,wu,wd,wup,wdn,g2)
+
+ORDER=("tr","dm","do","u","A","go","p0","0","v","p1","u","1","p2","0","2","B","p3","0","3","1","4","v","fo","fm","2","n","0","1","A","B","2","0","u","3","1","u","4","0","2","3","4","1","v","3","n","2","f","4","0","3","1","0","v","2","v","n","4","3","n","1","4","1","2","2","3","4","3","4","n")
+EARLY_X=(2,)
+
+class Wires:
+    def __init__(self,sems):
+        self.sems=sems; self.count=0; self.all=[]
+    def send(self,src,dst,dev):
+        k=remote(src,dst,self.sems,self.count,dev)
+        self.count+=1
+        k.start()
+        self.all.append(k)
+        return k
+
+def k3_kernel(dbr,tok,rows_i,wqkv,wf,wout,proj_i,feat_i,mixed_i,rden_i,g1,dmid_i,mid_i,mlp_i,gu_i,gd_i,gn2,
+              bo_o,gt_o,go_o,gp_o,gu_o,gd_o,gn_o,
+              db,T,rows,rowsT,gsum,wq,wo,proj,feat,mixed,rden,datt,dproj,dmid,mid,
+              G0,GP,C0,CP,X0,XP,U0,UP,W0,WP,
+              GU,GD,zd,yu,yd,ML,ma,mb,na,nb,bo,dfo,dfs,dfr,gt,gn,gr,w2,loc,sems):
+    x,c,y,z=place()
+    nx,ny,nc=around()
+    nh=lax.axis_size("hidden")
+    z1,z2=z+1-2*(z%2),(z+2)%nh
+    n1=(x*2+c,y,z1); n2=(x*2+c,y,z2)
+    R=dbr.shape[0]; n=2*R; d=dbr.shape[1]; H=R//2
+    hd=wf.shape[-1]; w=2*hd; pairs=w2.shape[1]; nz=gd_i.shape[0]; fs=gu_i.shape[2]
+    qo,qx,qy,qd=x*2+y,(1-x)*2+y,x*2+1-y,(1-x)*2+1-y
+    mine=pl.ds(pl.multiple_of(y*R,R),R); other=pl.ds(pl.multiple_of((1-y)*R,R),R)
+    A=pl.ds(0,H); B=pl.ds(H,H)
+    half=lambda size,b: pl.ds(pl.multiple_of(b*size,size),size)
+    nloc=[0]; pend=[]
+    def lc(s,t,out=False):
+        k=pltpu.make_async_copy(s,t,loc.at[nloc[0]]); nloc[0]+=1
+        k.start()
+        if out: pend.append(k)
+        return k
+    wires=Wires(sems)
+    send=wires.send
+    hu,hw=d//2,fs//2
+    l_db=lc(dbr,db.at[mine]); l_wo=lc(wout,wo); l_rows=lc(rows_i,rows)
+    greet((nx,ny,nc,n1,n2),False)
+    r_db=send(dbr,db.at[mine],ny)
+    l_gu=lc(gu_i,GU); l_gd=lc(gd_i,GD)
+    l_feat=lc(feat_i,feat); l_proj=lc(proj_i,proj); l_mixed=lc(mixed_i,mixed); l_rden=lc(rden_i,rden)
+    l_wq=lc(wqkv,wq); l_ml=lc(mlp_i,ML); l_T=lc(tok,T); l_dm=lc(dmid_i,dmid); l_mid=lc(mid_i,mid)
+    pair_weights(wf,w2)
+    ones=half_ones(2*w,hd); ones1=half_ones(w,hd)
+
+    def grads(G,bufs,O,back=(3,2,1,0)):
+        steps=[(nc,c),(nx,x),(n1,z%2),(n2,z//2)]
+        size=G.shape[0]; base=0
+        for (dev,bit),buf in zip(steps,bufs):
+            size//=2
+            away=pl.multiple_of(base+(1-bit)*size,16)
+            base=pl.multiple_of(base+bit*size,16)
+            k=send(G.at[pl.ds(away,size)],buf,dev)
+            yield
+            k.wait_recv()
+            add_into(G.at[pl.ds(base,size)],buf,size//2 if size%32==0 else size)
+        src=G.at[pl.ds(base,size)]
+        own=lc(src,O.at[c,x,z%2,z//2])
+        at=[c,x,z%2,z//2]
+        for i in back:
+            ref=lambda: O.at[tuple(at)]
+            k=send(ref() if src is None else src,ref(),steps[i][0])
+            src=None
+            yield
+            k.wait_recv()
+            if own is not None: own.wait()
+            own=None
+            at[i]=slice(None)
+
+    def mlp_grads(first,near,later,last,own,piece,rows):
+        first.wait()
+        if later is not None:
+            k=[send(near(z1),later.at[0],n1),send(near((z1+2)%nh),later.at[1],n1)]
+            yield
+            for t in k: t.wait_recv()
+            add_into(near(z2),later.at[1],rows)
+        k=send(near(z2),last,n2)
+        if later is not None: add_into(near(z),later.at[0],rows)
+        yield
+        k.wait_recv()
+        mine_=near(z)
+        add_into(mine_,last,rows)
+        l=lc(mine_,piece(qo))
+        k=send(mine_,piece(qo),nx)
+        k2=send(mine_,piece(qo),ny)
+        yield
+        k.wait_recv()
+        k=send(piece(qx),piece(qx),ny)
+        yield
+        k.wait_recv(); k2.wait_recv(); l.wait()
+        k=send(own,own,nc)
+        yield
+        k.wait_recv()
+
+    def mlp_rows(at,near,dev,q1,q2,buf,far,q3):
+        k=[send(mlp_i.at[q1,at],buf.at[0],near),send(mlp_i.at[q2,at],buf.at[1],near)]
+        yield
+        l_ml.wait() if at is A else None
+        for t in k: t.wait_recv()
+        add_into(ML.at[qo,at],buf.at[0],H); add_into(ML.at[q3,at],buf.at[1],H)
+        k=send(ML.at[q3,at],far,dev)
+        yield
+        k.wait_recv()
+        if at is A: l_mid.wait()
+        bo[at]=(mid[at]+(ML[qo,at].astype(F32)+far[...].astype(F32))).astype(BF)
+        lc(bo.at[at],bo_o.at[at],True)
+
+    def first_grad(at):
+        t=mm_nt(dproj[0,at],wq[0])+mm_nt(dproj[1,at],wq[1])
+        return t+mm_nt(dproj[2,at],wq[2])
+
+    def first_rows():
+        l_wq.wait()
+        t=first_grad(other)
+        dfs[...]=t.astype(BF)
+        k=send(dfs,dfr,ny)
+        l_T.wait()
+        xo,_=unit(T[other].astype(F32))
+        gsum[...]=jnp.sum(t*xo,axis=0,keepdims=True)
+        yield
+        k.wait_recv()
+        l_dm.wait()
+        dx,_=norm_back(T[mine].astype(F32),dfo[...]+dfr[...].astype(F32),g1[...])
+        gt[...]=dmid[...]+dx
+        lc(gt,gt_o,True)
+
+    def gains():
+        t=first_grad(mine)
+        dfo[...]=t
+        xm,_=unit(T[mine].astype(F32))
+        gn[...]=jnp.zeros_like(gn)
+        gn[0,0:1]=gsum[...]+jnp.sum(t*xm,axis=0,keepdims=True)
+        gn[0,1:2]=gn2[...]
+        order=[nc,nx,ny,n1,n2]
+        for i,dev in enumerate(order):
+            k=send(gn.at[i],gr.at[i],dev)
+            yield
+            k.wait_recv()
+            gn[i+1]=gn[i]+gr[i]
+        gn_o[...]=gn[len(order)]
+
+    def pair(p):
+        cc=slice(p*w,(p+1)*w)
+        fq=feat[0,p]; fk=feat[1,p]
+        dfq,dfk,dv=attend_back(fq,fk,proj[2,:,cc],mixed[:,cc],rden[:,cc],datt[:,cc],ones1,hd)
+        parts=[]
+        for t,(f,df) in enumerate(((fq,dfq),(fk,dfk))):
+            du=feature_back(f,df,ones)
+            GP[p,pl.ds(3*d+t*w,w)]=mm_tn(proj[t,:,cc],du).astype(BF)
+            parts.append(mm_nt(du,w2[t,p]).astype(BF))
+        parts.append(dv.astype(BF))
+        for t in range(3): dproj[t,:,cc]=parts[t]
+        g=mm(rowsT[...],jnp.concatenate(parts,axis=1)).astype(BF)
+        for t in range(3): GP[p,pl.ds(t*d,d)]=g[:,t*w:(t+1)*w]
+
+    uh=half(hu,c)
+    qc=lambda q: pl.ds(pl.multiple_of(q*fs,fs),fs)
+    chains={"0":grads(G0,(C0,X0,U0,W0),go_o),
+        "u":mlp_grads(l_gu,lambda j: GU.at[(j+nh-z)%nh//2],None,yu,gu_o.at[uh],lambda q: gu_o.at[uh,qc(q)],64),
+        "v":mlp_grads(l_gd,lambda j: GD.at[j],zd,yd,gd_o.at[:,half(hw,c)],lambda q: gd_o.at[q,half(hw,c)],16),
+        "A":mlp_rows(A,nx,ny,qx,qd,ma,na,qy),"B":mlp_rows(B,ny,nx,qy,qd,mb,nb,qx),
+        "f":first_rows(),"n":gains()}
+    for p in range(pairs): chains[str(p+1)]=grads(GP.at[p],(CP.at[p],XP.at[p],UP.at[p],WP.at[p]),gp_o.at[p],(1,3,2,0) if p in EARLY_X else (3,2,1,0))
+    def go(name): next(chains[name],None)
+    def do(name):
+        if name=="tr":
+            l_rows.wait()
+            rowsT[...]=rows[...].T
+        elif name=="dm":
+            l_db.wait(); l_wo.wait()
+            datt[mine]=mm_nt(db[mine],wo[...])
+        elif name=="do":
+            r_db.wait_recv()
+            go("B")
+            datt[other]=mm_nt(db[other],wo[...])
+        elif name=="go":
+            l_mixed.wait()
+            G0[...]=mm_tn(mixed[...],db[...]).astype(BF)
+            go("0")
+        elif name=="p0":
+            for k in (l_feat,l_proj,l_rden): k.wait()
+            pair(0); go("1")
+        elif name[0]=="p":
+            pair(int(name[1])); go(str(int(name[1])+1))
+        elif name=="fo": go("f")
+        elif name=="fm": go("n")
+        else: go(name)
+    for name in ("A","v","u"): go(name)
+    for name in ORDER: do(name)
+    for name in chains:
+        for _ in chains[name]: pass
+    for k in wires.all: k.wait_send()
+    for k in pend: k.wait()
+
+def k3(dbr,tok,rows,wqkv,wf,wout,proj,feat,mixed,rden,g1,dmid,mid,mlp,gu,gd,gn2):
+    R,d=dbr.shape; n=2*R; c=wout.shape[0]; h=wf.shape[1]; hd=wf.shape[-1]; pairs=h//2
+    nz=gd.shape[0]; fs=gu.shape[2]; f=nz*fs; w=2*hd; q=3*d+2*w
+    V=pltpu.VMEM; D=pltpu.SemaphoreType.DMA
+    like=lambda a: V(a.shape,a.dtype)
+    return pl.pallas_call(k3_kernel,
+      out_shape=(S((R,d),BF),S((R,d),F32),S((2,2,2,2,c//16,d),BF),S((pairs,2,2,2,2,q//16,w),BF),S((d,f),BF),S((4,fs,d),BF),S((8,d),F32)),
+      in_specs=[ANY,ANY,ANY,ANY,VM,ANY,ANY,ANY,ANY,ANY,VM,ANY,ANY,ANY,ANY,ANY,VM],
+      out_specs=[ANY]*6+[VM],
+      scratch_shapes=[V((n,d),BF),like(tok),like(rows),V((d,n),BF),V((1,d),F32),like(wqkv),like(wout),like(proj),like(feat),like(mixed),like(rden),
+        V((n,c),F32),like(proj),like(dmid),like(mid),
+        V((c,d),BF),V((pairs,q,w),BF),V((c//2,d),BF),V((pairs,q//2,w),BF),V((c//4,d),BF),V((pairs,q//4,w),BF),
+        V((c//8,d),BF),V((pairs,q//8,w),BF),V((c//16,d),BF),V((pairs,q//16,w),BF),
+        V((2,d//2,fs),BF),V((nz,fs//2,d),BF),V((2,fs//2,d),BF),
+        V((d//2,fs),BF),V((fs//2,d),BF),
+        like(mlp),V((2,R//2,d),BF),V((2,R//2,d),BF),V((R//2,d),BF),V((R//2,d),BF),V((R,d),BF),
+        V((R,d),F32),V((R,d),BF),V((R,d),BF),V((R,d),F32),V((6,8,d),F32),V((5,8,d),F32),
+        V((2,pairs,w,w),BF),D((40,)),D((2,80))],
+      compiler_params=pltpu.CompilerParams(vmem_limit_bytes=62*2**20,collective_id=3,has_side_effects=True),
+      cost_estimate=pl.CostEstimate(flops=8*10**9,bytes_accessed=40*10**6,transcendentals=10**6))(
+      dbr,tok,rows,wqkv,wf,wout,proj,feat,mixed,rden,g1,dmid,mid,mlp,gu,gd,gn2)
+
+def finish_kernel(go,g0,g1,g2,gf,gu,gd,go_o,gq_o,gf_o,gu_o,gd_o):
+    for a,b in ((go,go_o),(gu,gu_o),(gd,gd_o)): b[...]=a[...].astype(F32)
+    pairs,_,w=g0.shape; hd=w//2
+    for t,g in enumerate((g0,g1,g2)):
+        for p in range(pairs): gq_o[t,:,p*w:(p+1)*w]=g[p].astype(F32)
+    @pl.when(pl.program_id(0)==0)
+    def _():
+        for t in range(2):
+            for p in range(pairs):
+                for s in range(2):
+                    gf_o[t,2*p+s]=gf[p,t*w+s*hd:t*w+(s+1)*hd,s*hd:(s+1)*hd].astype(F32)
+
+def finish(go,gp,gu,gd,hd):
+    c,d=go.shape; pairs,_,w=gp.shape; f=gu.shape[1]; N=8
+    B=pl.BlockSpec
+    row=lambda a: B((a.shape[0]//N,a.shape[1]),lambda i:(i,0))
+    part=lambda t: B((pairs,d//N,w),lambda i:(0,i+N*t,0))
+    return pl.pallas_call(finish_kernel,grid=(N,),
+      out_shape=(S((c,d),F32),S((3,d,c),F32),S((2,2*pairs,hd,hd),F32),S((d,f),F32),S((f,d),F32)),
+      in_specs=[row(go),part(0),part(1),part(2),B((pairs,2*w,w),lambda i:(0,3*d//(2*w),0)),row(gu),row(gd)],
+      out_specs=[row(go),B((3,d//N,c),lambda i:(0,i,0)),B((2,2*pairs,hd,hd),lambda i:(0,0,0,0)),row(gu),row(gd)],
+      compiler_params=pltpu.CompilerParams(vmem_limit_bytes=62*2**20))(go,gp,gp,gp,gp,gu,gd)
 
 def per_device_k1(
     tokens, lengths, norm_first, w_qkv, w_feature, w_out, norm_second, w_up, w_down, cotangent
 ):
     wqkv=jnp.transpose(w_qkv,(1,0,2))
     tok,first_rows,proj,feat,mixed,rden,middle,second_low,wu,wd,cot_all=k1(lengths,tokens[0],norm_first[None],wqkv,w_feature,w_out,norm_second[None],w_up,w_down,cotangent[0])
-    residual_in = tokens[0].astype(jnp.float32)
-    _, first_back = jax.vjp(normalize, residual_in, norm_first)
-    cot_low = cotangent[0]
-    _, second_back = jax.vjp(normalize, middle, norm_second)
-    g=[[0,2],[1,3]]
-    sx=lax.all_gather(second_low,"dp",axis_index_groups=g)
-    sxy=lax.all_gather(sx,"head",axis=1).reshape(4*256,1024)
-    cot_rows=cot_all.reshape(1024,1024)
-    up=jnp.transpose(wu,(1,0,2)).reshape(1024,1024)
-    dn=wd.reshape(1024,1024)
-    hidden_pre = jnp.dot(sxy, up, preferred_element_type=jnp.float32)
-    active = smooth_gate(hidden_pre).astype(jnp.bfloat16)
-    gate_grad = jax.vjp(smooth_gate, hidden_pre)[1]
-    d_active = jnp.einsum("nd,fd->nf", cot_rows, dn, preferred_element_type=jnp.float32)
-    d_pre = gate_grad(d_active)[0].astype(jnp.bfloat16)
-    def scat(v):
-        v=v.astype(jnp.bfloat16).reshape(2,2,256,1024)
-        v=lax.psum_scatter(v,"head",scatter_dimension=1)
-        return lax.psum_scatter(v,"dp",scatter_dimension=0,axis_index_groups=g).astype(jnp.float32)
-    d_second=scat(jnp.einsum("nf,df->nd", d_pre, up, preferred_element_type=jnp.float32))
-    mlp_result=scat(jnp.dot(active, dn, preferred_element_type=jnp.float32))
-    block_out = (middle + mlp_result).astype(jnp.bfloat16)
-    gd = jnp.einsum("nf,nd->fd", active, cot_rows, preferred_element_type=jnp.float32).astype(BF).reshape(4,256,1024)
-    gu = jnp.einsum("nd,nf->df", sxy, d_pre, preferred_element_type=jnp.float32).astype(BF).reshape(1024,4,256)
-    gd=lax.psum_scatter(gd,"hidden",scatter_dimension=0)
-    gu=lax.psum_scatter(gu,"hidden",scatter_dimension=1)
-    gd=lax.psum(gd,"dp",axis_index_groups=[[0,1],[2,3]]); gu=lax.psum(gu,"dp",axis_index_groups=[[0,1],[2,3]])
-    grad_down=lax.all_gather(lax.all_gather(gd,"head"),"dp",axis_index_groups=g).reshape(1024,1024).astype(F32)
-    grad_up=lax.all_gather(lax.all_gather(gu,"head",axis=1),"dp",axis=1,axis_index_groups=g).reshape(1024,1024).astype(F32)
-    d_middle_norm, grad_norm_second = second_back(d_second)
-    d_middle = cot_low.astype(jnp.float32) + d_middle_norm
-    d_branch_rows = lax.all_gather(d_middle.astype(jnp.bfloat16), "head", axis=0, tiled=True)
-    gq,grad_feature,go,dfirst=bwd(first_rows,wqkv,w_feature,w_out,proj,feat,mixed,rden,d_branch_rows)
-    d_first = lax.psum_scatter(dfirst, "head", scatter_dimension=0, tiled=True).astype(jnp.float32)
-    d_input_norm, grad_norm_first = first_back(d_first)
-    grad_tokens = d_middle + d_input_norm
-    gq, grad_feature, go = (
-        lax.psum(gq, ("dp", "hidden")).astype(jnp.float32),
-        lax.psum(grad_feature.astype(jnp.bfloat16), ("dp", "hidden")).astype(jnp.float32),
-        lax.psum(go, ("dp", "hidden")).astype(jnp.float32),
-    )
-    grad_norm_first, grad_norm_second = lax.psum(
-        (grad_norm_first, grad_norm_second), ("dp", "head", "hidden")
-    )
+    d_middle,d_branch_low,gn2,mlp,gu,gd=k2(second_low,middle,cot_all,cotangent[0],wu,wd,w_up,w_down,norm_second[None])
+    block_out,grad_tokens,go,gp,gu,gd,gn=k3(d_branch_low,tok,first_rows,wqkv,w_feature,w_out,proj,feat,mixed,rden,norm_first[None],d_middle,middle,mlp,gu,gd,gn2)
+    d=tokens.shape[2]; h=w_feature.shape[1]; hd=w_feature.shape[3]; w=2*hd
+    go=go.reshape(w_out.shape); gp=gp.reshape(h//2,-1,w)
+    go,gq,gf,gu,gd=finish(go,gp,gu,gd.reshape(gd.shape[0]*gd.shape[1],-1),hd)
     return (
         block_out[None],
         grad_tokens[None],
-        grad_norm_first,
+        gn[0],
         jnp.transpose(gq,(1,0,2)),
-        grad_feature,
+        gf,
         go,
-        grad_norm_second,
-        grad_up,
-        grad_down,
+        gn[1],
+        gu,
+        gd,
     )
 
 

time: 655 us -> 202 us (0.31)
  waiting for transfers between devices: 435 us -> 0 us
  Pallas kernels: 71.6 us -> 194 us
  blocking collectives: 40.9 us -> 0 us
  matrix products: 33.7 us -> 0 us
  other arithmetic: 29.3 us -> 0 us
  local copies, waits for them, and re-layouts: 27.3 us -> 3.21 us
  between operations: 14.7 us -> 1.76 us
    reduce_scatter x7 -> x0, waiting for transfers between devices: 198 us -> none  [the longest x2 68.3 us: scat(): v = lax.psum_scatter(v, 'head', scatter_dimension=1)]
    all_gather x7 -> x0, waiting for transfers between devices: 141 us -> none  [the longest x1 24.8 us: per_device_k1(): sxy = lax.all_gather(sx, 'head', axis=1).reshape(4 * 256, 1024)]
    pallas_call x1 -> x3, Pallas kernels: 22.7 us -> 148 us  [the longest x1 93.2 us: k3(): pl.pallas_call(k3_kernel, out_shape=(S((R, d), BF), S((R, d), F32), S((2,...]
    psum x2 -> x0, waiting for transfers between devices: 95.6 us -> none  [the longest x1 73.6 us: per_device_k1(): lax.psum(gq, ('dp', 'hidden')).astype(jnp.float32)]
    psum x1 -> x0, blocking collectives: 40.9 us -> none  [per_device_k1(): lax.psum((grad_norm_first, grad_norm_second), ('dp', 'head', 'hidden'))]
    dot_general x6 -> x0, matrix products: 33.7 us -> none  [the longest x1 8.29 us: per_device_k1(): hidden_pre = jnp.dot(sxy, up, preferred_element_type=jnp.float32)]
    convert_element_type x6 -> x0, other arithmetic: 15.6 us -> none  [the longest x1 4.07 us: per_device_k1(): lax.all_gather(lax.all_gather(gu, 'head', axis=1), 'dp', axis=1, axis_ind...]
    unnamed x35 -> x6, local copies, waits for them, and re-layouts: 13.4 us -> 1.77 us
  transfers between devices with their start and end apart: 16 -> 0, of which waited for: 16 -> 0; matrix products, arithmetic and copies ran while one was open for 9% -> 0% of each run, Pallas kernels for 3% -> 0%
where the time goes in v3:
time: 202 us; the launch traced here: 199 us
  Pallas kernels  194 us (96%)
  local copies, waits for them, and re-layouts  3.21 us (2%)
    pallas_call x1, Pallas kernels, k3(): pl.pallas_call(k3_kernel, out_shape=(S((R, d), BF), S((R, d), F32), S((2,...  93.2 us
    pallas_call x1, Pallas kernels, k1(): pl.pallas_call(k1_kernel, out_shape=tuple(big + [S((last + 1, d, f // 4),...  45.3 us
    pallas_call x1, Pallas kernels, k2(): pl.pallas_call(k2_kernel, out_shape=(S((R, d), F32), S((R, d), BF), S((1,...  44 us
    pallas_call x1, Pallas kernels, finish(): pl.pallas_call(finish_kernel, grid=(N,), out_shape=(S((c, d), F32), S((3,...  11.2 us

profile of v3, /device:TPU:0, one launch (start us, length us, event | category | flops | bytes accessed | tf_op | source)
XLA Modules:
  0.0 198.7 jit_solution(1593076214294929264)
XLA Ops:
  1.3 45.3 %shard_map.169 = (bf16[512,1024]{1,0:T(8,128)(2,1)}, bf16[512,1024]{1,0:T(8,128)(2,1)}, bf16[3,512,512]{2,1,0:T(8,128)(2,1)}, bf16[2,4,512,256]{3,2,1,0:T(8,128)...) custom-call(s32[1,1]{1,0:T(1,128)S(6)} %copy.21.len_ref, ...), custom_call_target="tpu_custom_call" | custom-call | flops 4000000000 | bytes 30000000 | tf_op jit(solution)/shard_map/pallas_call | solution.py:427
  46.6 44.0 %shard_map.170 = (f32[256,1024]{1,0:T(8,128)}, bf16[256,1024]{1,0:T(8,128)(2,1)}, f32[1,1024]{1,0:T(1,128)}, bf16[4,256,1024]{2,1,0:T(8,128)(2,1)}, bf16[2,512,2...) custom-call(bf16[256,1024]{1,0:T(8,128)(2,1)} %get-tuple-element.38.sec, f32[256,1024]{1,0:T(8,128)} %get-tuple-element.39.mid.mid_i, ...), custom_call_target="tpu_custom_call" | custom-call | flops 12999999488 | bytes 30000000 | tf_op jit(solution)/shard_map/pallas_call | solution.py:565
  90.6 93.2 %shard_map.171 = (bf16[256,1024]{1,0:T(8,128)(2,1)}, f32[256,1024]{1,0:T(8,128)}, bf16[2,2,2,2,32,1024]{5,4,3,2,1,0:T(8,128)(2,1)}, bf16[4,2,2,2,2,208,128]{6,5,...) custom-call(bf16[256,1024]{1,0:T(8,128)(2,1)} %get-tuple-element.43.dbr, ...), custom_call_target="tpu_custom_call" | custom-call | flops 8000000000 | bytes 40000000 | tf_op jit(solution)/shard_map/pallas_call | solution.py:777
  183.8 1.4 fusion
  185.2 0.0 copy-start.1
  185.2 0.0 copy-start
  185.2 11.2 %shard_map.172 = (f32[512,1024]{1,0:T(8,128)}, f32[3,1024,512]{2,1,0:T(8,128)}, f32[2,8,64,64]{3,2,1,0:T(8,128)}, f32[1024,1024]{1,0:T(8,128)}, f32[1024,1024]{1,0:T(8,128)}) custom-call(bf16[512,1024]{1,0:T(8,128)(2,1)} %bitcast.18, bf16[4,3328,128]{2,1,0:T(8,128)(2,1)} %bitcast.13, bf16[4,3328,128]{2,1,0:T(8,128)(2,1)} %bitcast.14, ...), custom_call_target="tpu_custom_call" | custom-call | tf_op jit(solution)/shard_map/pallas_call | solution.py:811
  196.5 0.0 copy-done.1
  196.5 0.8 copy.22
  197.3 0.0 copy-done
  197.3 1.0 copy.23
Async XLA Ops:
  185.2 11.2 %copy-start.1 = (bf16[256,1024]{1,0:T(8,128)(2,1)S(1)}, bf16[256,1024]{1,0:T(8,128)(2,1)}, u32[]{:S(2)}) copy-start(bf16[256,1024]{1,0:T(8,128)(2,1)} %get-tuple-element.55) | copy-start | bytes 1572868
  185.2 12.0 %copy-start = (f32[256,1024]{1,0:T(8,128)S(1)}, f32[256,1024]{1,0:T(8,128)}, u32[]{:S(2)}) copy-start(f32[256,1024]{1,0:T(8,128)} %get-tuple-element.56) | copy-start | bytes 3145732
